TPU v7x, 512 devices: a whole 4x4x16 slice. The times are simulated.
512 devices in a mesh: cuts: 16 (over z_lo, y), energy: 32 (over x, z_hi, core).
Axes of the slice: x: 4, y: 4, z: 16 (z_hi: 4, z_lo: 4; z = z_hi * 4 + z_lo), core: 2. Of those that a mesh axis runs over, the one named last changes fastest.
Arguments:
- inverse: bfloat16 [2, 64, 16, 512, 512], P(None, 'energy', 'cuts'), may hold values from -3 to 3
- coupling: bfloat16 [2, 16, 512, 512], P(None, 'cuts'), may hold values from -0.15625 to 0.15625
- pattern: int32 [16, 4, 4], P('cuts'), may hold values 0 or 1
- source: bfloat16 [2, 64, 16, 96, 512], P(None, 'energy', 'cuts'), may hold values from -6 to 6
- previous: bfloat16 [2, 64, 16, 96, 512], P(None, 'energy', 'cuts'), may hold values from -6 to 6
- offsets: int32 [4], replicated, may hold values from 1 to 2, as said below
- strength: float32 [4], replicated, may hold values from 0.2 to 0.5
Outputs:
- updated: bfloat16 [2, 64, 16, 96, 512], P(None, 'energy', 'cuts')
Inputs may be any that keep to these rules, and one draw needn't show every extreme that they name: One of the offsets equals 2.
All inputs are finite; a program needn't handle non-finite values. No bound on the sum of `pattern` on one device may be relied on, other than what follows from the above.
Results may differ from a plain program's by a relative error of at most 0.035.
Values may be sent and summed in bfloat16 or wider, within the bound.
A program may use at most 64 MiB of HBM per device.

v0:
```python
import jax
import jax.numpy as jnp
from jax import lax
from jax.sharding import PartitionSpec as P


def padded_2(cells, sides, width):
    for axis, dim in sides:
        count = lax.axis_size(axis)
        ends = count - 1
        head = lax.slice_in_dim(cells, 0, width, axis=dim)
        tail = lax.slice_in_dim(cells, cells.shape[dim] - width, cells.shape[dim], axis=dim)
        cells = jnp.concatenate(
            [
                lax.ppermute(tail, axis, [(i, (i + 1) % count) for i in range(ends)]),
                cells,
                lax.ppermute(head, axis, [((i + 1) % count, i) for i in range(ends)]),
            ],
            axis=dim,
        )
    return cells


def passed_along(value, axis, steps):
    count = lax.axis_size(axis)
    leading, last = (max(0, -steps), min(count, count - steps))
    return lax.ppermute(value, axis, [(source, source + steps) for source in range(leading, last)])


def expand_pattern(coupling, pattern):
    blocks = pattern.shape[-1]
    block_width = coupling.shape[-1] // blocks
    shaped = coupling.reshape(coupling.shape[:-2] + (blocks, block_width, blocks, block_width))
    block_mask = pattern.astype(coupling.dtype)[..., :, None, :, None]
    return (shaped * block_mask).reshape(coupling.shape)


def times_inverse(matrix, vector):
    with_real = jnp.einsum("cero,epo->cerp", vector, matrix[0], preferred_element_type=jnp.float32)
    with_imag = jnp.einsum("cero,epo->cerp", vector, matrix[1], preferred_element_type=jnp.float32)
    return jnp.stack([with_real[0] - with_imag[1], with_real[1] + with_imag[0]])


def couple(matrix, vector):
    with_real = jnp.einsum("cero,po->cerp", vector, matrix[0], preferred_element_type=jnp.float32)
    with_imag = jnp.einsum("cero,po->cerp", vector, matrix[1], preferred_element_type=jnp.float32)
    return jnp.stack([with_real[0] - with_imag[1], with_real[1] + with_imag[0]])


def couple_adjoint(matrix, vector):
    with_real = jnp.einsum("cero,op->cerp", vector, matrix[0], preferred_element_type=jnp.float32)
    with_imag = jnp.einsum("cero,op->cerp", vector, matrix[1], preferred_element_type=jnp.float32)
    return jnp.stack([with_real[0] + with_imag[1], with_real[1] - with_imag[0]])


def forward_local(incoming, drive_term, inverse, masked):
    carried_state = incoming
    step_term = drive_term[:, :, 0].astype(jnp.float32) - couple(masked[:, 0], carried_state)
    step_term = step_term.astype(jnp.bfloat16)
    carried_state = times_inverse(inverse[:, :, 0], step_term).astype(jnp.bfloat16)
    stored = [carried_state]
    return (jnp.stack(stored, axis=2), carried_state)


def backward_local(incoming, forward, inverse, masked):
    carried = incoming
    slices_here = inverse.shape[2]
    stored = [None] * slices_here
    for cut_index in reversed(range(slices_here)):
        newest = forward[:, :, cut_index].astype(jnp.float32) - times_inverse(
            inverse[:, :, cut_index], carried
        )
        newest = newest.astype(jnp.bfloat16)
        stored[cut_index] = newest
        carried = couple_adjoint(masked[:, cut_index], newest).astype(jnp.bfloat16)
    return (jnp.stack(stored, axis=2), carried)


def on_device(inverse, coupling, pattern, source, previous, offsets, strength):
    energies_here = inverse.shape[1]
    state_rows = source.shape[3]
    orbitals = source.shape[4]
    padded = padded_2(previous, (("energy", 1),), energies_here)
    summed = source.astype(jnp.float32)
    for channel in range(offsets.shape[0]):
        offset_now = offsets[channel]
        above_energy = lax.dynamic_slice_in_dim(
            padded, energies_here + offset_now, energies_here, 1
        )
        below_energy = lax.dynamic_slice_in_dim(
            padded, energies_here - offset_now, energies_here, 1
        )
        summed = summed + strength[channel] * (
            above_energy.astype(jnp.float32) + below_energy.astype(jnp.float32)
        )
    drive_term = summed.astype(jnp.bfloat16)
    masked = expand_pattern(coupling, pattern[None])
    places = lax.axis_size("cuts")
    position = lax.axis_index("cuts")
    full_zeros = jnp.zeros(source.shape, jnp.bfloat16)
    edge_zeros = jnp.zeros((2, energies_here, state_rows, orbitals), jnp.bfloat16)

    def forward_turn(turn, carry):
        stored, outgoing = carry
        incoming = passed_along(outgoing, "cuts", 1)
        return lax.cond(
            turn == position,
            lambda: forward_local(incoming, drive_term, inverse, masked),
            lambda: (stored, outgoing),
        )

    forward, _ = lax.fori_loop(0, places, forward_turn, (full_zeros, edge_zeros))

    def backward_turn(turn, carry):
        stored, outgoing = carry
        incoming = passed_along(outgoing, "cuts", -1)
        return lax.cond(
            turn == places - 1 - position,
            lambda: backward_local(incoming, forward, inverse, masked),
            lambda: (stored, outgoing),
        )

    result, _ = lax.fori_loop(0, places, backward_turn, (full_zeros, edge_zeros))
    return result


def solution(mesh):
    return jax.shard_map(
        on_device,
        mesh=mesh,
        in_specs=(
            P(None, "energy", "cuts", None, None),
            P(None, "cuts", None, None),
            P("cuts", None, None),
            P(None, "energy", "cuts", None, None),
            P(None, "energy", "cuts", None, None),
            P(),
            P(),
        ),
        out_specs=P(None, "energy", "cuts", None, None),
        check_vma=False,
    )
```

profile of v0, /device:TPU:6, one launch (start us, length us, event | category | flops | bytes accessed | tf_op | source)
XLA Modules:
  0.0 809.9 jit_solution(6337237430986404383)
XLA Ops:
  0.0 2.0 collective-permute-start.2
  2.1 12.4 %collective-permute-start.3 = (bf16[2,2,1,96,512]{4,3,1,0,2:T(8,128)(2,1)}, bf16[2,2,1,96,512]{4,3,1,0,2:T(8,128)(2,1)S(1)}, u32[]{:S(2)}, u32[]{:S(2)}) collective-permute-start(bf16[2,2,1,96,512]{4,3,1,0,2:T(8,128)(2,1)} %bitcast.113), channel_id=1, source_target_pairs={{1,0},{2,1},{3,2},{4,3},{5,4},{6,5},{7,6},{8,7},{9,8},{10,9},{11,1... | collective-permute-start | bytes 1179656 | tf_op jit(solution)/shard_map/ppermute | solution.py:17
  29.9 3.3 add_convert_fusion
  34.7 294.5 %while.32 = (s32[]{:T(128)}, bf16[2,2,1,96,512]{4,3,1,2,0:T(8,128)(2,1)}, bf16[2,2,96,512]{3,2,0,1:T(8,128)(2,1)}, s32[]{:T(128)}, bf16[2,2,1,96,512]{4,3,1,0,2:...) while((s32[]{:T(128)}, ...), condition=%wide.region_3.0_spmd, body=%wide.region_0.0_spmd.sunk | while | flops 807862272 | bytes 25034992 | solution.py:112
  34.8 1.8 copy.41
  36.5 4.2 collective-permute-start
  40.7 4.8 collective-permute-done
  45.6 12.4 %conditional.4 = ((bf16[2,2,1,96,512]{4,3,1,2,0:T(8,128)(2,1)}, bf16[2,2,96,512]{3,2,0,1:T(8,128)(2,1)})) conditional(s32[]{:T(128)} %convert_element_type.123, (bf16[2,2,1,96,512]{4,3,1,2,0:T(8,128)(2,1)}, bf16[2,2,96,512]{3,2,0,1:T(8,128)(2,1)}) %tuple.88, (bf16[2,2,1,96,512]{4,3,1,0,2:T(8,128)(2,1)S(1)}, ...), branch_computations={%region_1.0_spmd, %region_2.0_spmd} | conditional | flops 807862272 | bytes 22675508 | solution.py:106
  46.9 2.0 reshape.118
  48.9 2.4 fusion.5
  51.4 2.0 reshape.117
  59.8 2.0 collective-permute-start
  61.8 4.9 collective-permute-done
  66.7 1.8 copy.41
  68.4 17.6 %collective-permute-start = (bf16[2,2,96,512]{3,2,1,0:T(8,128)(2,1)}, bf16[2,2,96,512]{3,2,1,0:T(8,128)(2,1)}, u32[]{:S(2)}, u32[]{:S(2)}) collective-permute-start(bf16[2,2,96,512]{3,2,1,0:T(8,128)(2,1)} %copy.41), channel_id=1, source_target_pairs={{0,32},{32,64},{64,96},{96,128},{128,160},{160,192},{192,224},{224... | collective-permute-start | bytes 1179656 | tf_op jit(solution)/shard_map/while/body/eval_jaxpr/ppermute | solution.py:27
  86.0 6.0 collective-permute-done
  93.7 5.1 collective-permute-start
  98.8 7.0 collective-permute-done
  105.9 1.8 copy.41
  107.6 14.5 %collective-permute-start = (bf16[2,2,96,512]{3,2,1,0:T(8,128)(2,1)}, bf16[2,2,96,512]{3,2,1,0:T(8,128)(2,1)}, u32[]{:S(2)}, u32[]{:S(2)}) collective-permute-start(bf16[2,2,96,512]{3,2,1,0:T(8,128)(2,1)} %copy.41), channel_id=1, source_target_pairs={{0,32},{32,64},{64,96},{96,128},{128,160},{160,192},{192,224},{224... | collective-permute-start | bytes 1179656 | tf_op jit(solution)/shard_map/while/body/eval_jaxpr/ppermute | solution.py:27
  122.2 7.6 collective-permute-done
  131.5 5.5 collective-permute-start
  137.0 8.7 %collective-permute-done = bf16[2,2,96,512]{3,2,1,0:T(8,128)(2,1)} collective-permute-done((bf16[2,2,96,512]{3,2,1,0:T(8,128)(2,1)}, bf16[2,2,96,512]{3,2,1,0:T(8,128)(2,1)}, u32[]{:S(2)}, u32[]{:S(2)}) %collective-permute-start) | collective-permute-done | bytes 393248 | tf_op jit(solution)/shard_map/while/body/eval_jaxpr/ppermute | solution.py:27
  147.5 14.2 %collective-permute-start = (bf16[2,2,96,512]{3,2,1,0:T(8,128)(2,1)}, bf16[2,2,96,512]{3,2,1,0:T(8,128)(2,1)}, u32[]{:S(2)}, u32[]{:S(2)}) collective-permute-start(bf16[2,2,96,512]{3,2,1,0:T(8,128)(2,1)} %copy.41), channel_id=1, source_target_pairs={{0,32},{32,64},{64,96},{96,128},{128,160},{160,192},{192,224},{224... | collective-permute-start | bytes 1179656 | tf_op jit(solution)/shard_map/while/body/eval_jaxpr/ppermute | solution.py:27
  161.7 8.8 %collective-permute-done = bf16[2,2,96,512]{3,2,1,0:T(8,128)(2,1)} collective-permute-done((bf16[2,2,96,512]{3,2,1,0:T(8,128)(2,1)}, bf16[2,2,96,512]{3,2,1,0:T(8,128)(2,1)}, u32[]{:S(2)}, u32[]{:S(2)}) %collective-permute-start) | collective-permute-done | bytes 393248 | tf_op jit(solution)/shard_map/while/body/eval_jaxpr/ppermute | solution.py:27
  172.2 5.1 collective-permute-start
  177.3 7.9 collective-permute-done
  187.0 16.9 %collective-permute-start = (bf16[2,2,96,512]{3,2,1,0:T(8,128)(2,1)}, bf16[2,2,96,512]{3,2,1,0:T(8,128)(2,1)}, u32[]{:S(2)}, u32[]{:S(2)}) collective-permute-start(bf16[2,2,96,512]{3,2,1,0:T(8,128)(2,1)} %copy.41), channel_id=1, source_target_pairs={{0,32},{32,64},{64,96},{96,128},{128,160},{160,192},{192,224},{224... | collective-permute-start | bytes 1179656 | tf_op jit(solution)/shard_map/while/body/eval_jaxpr/ppermute | solution.py:27
  203.9 7.0 collective-permute-done
  212.7 6.6 collective-permute-start
  219.3 5.9 collective-permute-done
  227.0 13.7 %collective-permute-start = (bf16[2,2,96,512]{3,2,1,0:T(8,128)(2,1)}, bf16[2,2,96,512]{3,2,1,0:T(8,128)(2,1)}, u32[]{:S(2)}, u32[]{:S(2)}) collective-permute-start(bf16[2,2,96,512]{3,2,1,0:T(8,128)(2,1)} %copy.41), channel_id=1, source_target_pairs={{0,32},{32,64},{64,96},{96,128},{128,160},{160,192},{192,224},{224... | collective-permute-start | bytes 1179656 | tf_op jit(solution)/shard_map/while/body/eval_jaxpr/ppermute | solution.py:27
  240.6 5.2 collective-permute-done
  247.6 7.2 collective-permute-start
  254.9 4.8 collective-permute-done
  261.5 14.3 %collective-permute-start = (bf16[2,2,96,512]{3,2,1,0:T(8,128)(2,1)}, bf16[2,2,96,512]{3,2,1,0:T(8,128)(2,1)}, u32[]{:S(2)}, u32[]{:S(2)}) collective-permute-start(bf16[2,2,96,512]{3,2,1,0:T(8,128)(2,1)} %copy.41), channel_id=1, source_target_pairs={{0,32},{32,64},{64,96},{96,128},{128,160},{160,192},{192,224},{224... | collective-permute-start | bytes 1179656 | tf_op jit(solution)/shard_map/while/body/eval_jaxpr/ppermute | solution.py:27
  275.8 4.8 collective-permute-done
  282.4 7.2 collective-permute-start
  289.6 4.8 collective-permute-done
  296.2 14.3 %collective-permute-start = (bf16[2,2,96,512]{3,2,1,0:T(8,128)(2,1)}, bf16[2,2,96,512]{3,2,1,0:T(8,128)(2,1)}, u32[]{:S(2)}, u32[]{:S(2)}) collective-permute-start(bf16[2,2,96,512]{3,2,1,0:T(8,128)(2,1)} %copy.41), channel_id=1, source_target_pairs={{0,32},{32,64},{64,96},{96,128},{128,160},{160,192},{192,224},{224... | collective-permute-start | bytes 1179656 | tf_op jit(solution)/shard_map/while/body/eval_jaxpr/ppermute | solution.py:27
  310.6 4.8 collective-permute-done
  317.2 7.2 collective-permute-start
  324.4 4.8 collective-permute-done
  330.1 479.9 %while.33 = (s32[]{:T(128)}, bf16[2,2,1,96,512]{4,3,1,2,0:T(8,128)(2,1)}, bf16[2,2,96,512]{3,2,1,0:T(8,128)(2,1)S(1)}, s32[]{:T(128)}, bf16[2,2,1,96,512]{4,3,1,...) while((s32[]{:T(128)}, ...), condition=%wide.region_7.0_spmd, body=%wide.region_4.0_spmd.sunk | while | flops 806879232 | bytes 25821452 | solution.py:123
  332.1 20.3 %collective-permute-done.1 = bf16[2,2,96,512]{3,2,0,1:T(8,128)(2,1)} collective-permute-done((bf16[2,2,96,512]{3,2,0,1:T(8,128)(2,1)}, bf16[2,2,96,512]{3,2,0,1:T(8,128)(2,1)}, u32[]{:S(2)}, u32[]{:S(2)}) %collective-permute-start.1) | collective-permute-done | bytes 393248 | tf_op jit(solution)/shard_map/while/body/eval_jaxpr/ppermute | solution.py:27
  354.5 11.3 %collective-permute-done.1 = bf16[2,2,96,512]{3,2,0,1:T(8,128)(2,1)} collective-permute-done((bf16[2,2,96,512]{3,2,0,1:T(8,128)(2,1)}, bf16[2,2,96,512]{3,2,0,1:T(8,128)(2,1)}, u32[]{:S(2)}, u32[]{:S(2)}) %collective-permute-start.1) | collective-permute-done | bytes 393248 | tf_op jit(solution)/shard_map/while/body/eval_jaxpr/ppermute | solution.py:27
  367.8 18.9 %collective-permute-done.1 = bf16[2,2,96,512]{3,2,0,1:T(8,128)(2,1)} collective-permute-done((bf16[2,2,96,512]{3,2,0,1:T(8,128)(2,1)}, bf16[2,2,96,512]{3,2,0,1:T(8,128)(2,1)}, u32[]{:S(2)}, u32[]{:S(2)}) %collective-permute-start.1) | collective-permute-done | bytes 393248 | tf_op jit(solution)/shard_map/while/body/eval_jaxpr/ppermute | solution.py:27
  388.8 10.2 %collective-permute-done.1 = bf16[2,2,96,512]{3,2,0,1:T(8,128)(2,1)} collective-permute-done((bf16[2,2,96,512]{3,2,0,1:T(8,128)(2,1)}, bf16[2,2,96,512]{3,2,0,1:T(8,128)(2,1)}, u32[]{:S(2)}, u32[]{:S(2)}) %collective-permute-start.1) | collective-permute-done | bytes 393248 | tf_op jit(solution)/shard_map/while/body/eval_jaxpr/ppermute | solution.py:27
  401.0 23.2 %collective-permute-done.1 = bf16[2,2,96,512]{3,2,0,1:T(8,128)(2,1)} collective-permute-done((bf16[2,2,96,512]{3,2,0,1:T(8,128)(2,1)}, bf16[2,2,96,512]{3,2,0,1:T(8,128)(2,1)}, u32[]{:S(2)}, u32[]{:S(2)}) %collective-permute-start.1) | collective-permute-done | bytes 393248 | tf_op jit(solution)/shard_map/while/body/eval_jaxpr/ppermute | solution.py:27
  426.3 8.7 %collective-permute-done.1 = bf16[2,2,96,512]{3,2,0,1:T(8,128)(2,1)} collective-permute-done((bf16[2,2,96,512]{3,2,0,1:T(8,128)(2,1)}, bf16[2,2,96,512]{3,2,0,1:T(8,128)(2,1)}, u32[]{:S(2)}, u32[]{:S(2)}) %collective-permute-start.1) | collective-permute-done | bytes 393248 | tf_op jit(solution)/shard_map/while/body/eval_jaxpr/ppermute | solution.py:27
  437.1 26.7 %collective-permute-done.1 = bf16[2,2,96,512]{3,2,0,1:T(8,128)(2,1)} collective-permute-done((bf16[2,2,96,512]{3,2,0,1:T(8,128)(2,1)}, bf16[2,2,96,512]{3,2,0,1:T(8,128)(2,1)}, u32[]{:S(2)}, u32[]{:S(2)}) %collective-permute-start.1) | collective-permute-done | bytes 393248 | tf_op jit(solution)/shard_map/while/body/eval_jaxpr/ppermute | solution.py:27
  465.9 12.1 %collective-permute-done.1 = bf16[2,2,96,512]{3,2,0,1:T(8,128)(2,1)} collective-permute-done((bf16[2,2,96,512]{3,2,0,1:T(8,128)(2,1)}, bf16[2,2,96,512]{3,2,0,1:T(8,128)(2,1)}, u32[]{:S(2)}, u32[]{:S(2)}) %collective-permute-start.1) | collective-permute-done | bytes 393248 | tf_op jit(solution)/shard_map/while/body/eval_jaxpr/ppermute | solution.py:27
  480.0 24.1 %collective-permute-done.1 = bf16[2,2,96,512]{3,2,0,1:T(8,128)(2,1)} collective-permute-done((bf16[2,2,96,512]{3,2,0,1:T(8,128)(2,1)}, bf16[2,2,96,512]{3,2,0,1:T(8,128)(2,1)}, u32[]{:S(2)}, u32[]{:S(2)}) %collective-permute-start.1) | collective-permute-done | bytes 393248 | tf_op jit(solution)/shard_map/while/body/eval_jaxpr/ppermute | solution.py:27
  506.1 13.5 %collective-permute-done.1 = bf16[2,2,96,512]{3,2,0,1:T(8,128)(2,1)} collective-permute-done((bf16[2,2,96,512]{3,2,0,1:T(8,128)(2,1)}, bf16[2,2,96,512]{3,2,0,1:T(8,128)(2,1)}, u32[]{:S(2)}, u32[]{:S(2)}) %collective-permute-start.1) | collective-permute-done | bytes 393248 | tf_op jit(solution)/shard_map/while/body/eval_jaxpr/ppermute | solution.py:27
  521.7 19.4 %collective-permute-done.1 = bf16[2,2,96,512]{3,2,0,1:T(8,128)(2,1)} collective-permute-done((bf16[2,2,96,512]{3,2,0,1:T(8,128)(2,1)}, bf16[2,2,96,512]{3,2,0,1:T(8,128)(2,1)}, u32[]{:S(2)}, u32[]{:S(2)}) %collective-permute-start.1) | collective-permute-done | bytes 393248 | tf_op jit(solution)/shard_map/while/body/eval_jaxpr/ppermute | solution.py:27
  543.1 10.9 %collective-permute-done.1 = bf16[2,2,96,512]{3,2,0,1:T(8,128)(2,1)} collective-permute-done((bf16[2,2,96,512]{3,2,0,1:T(8,128)(2,1)}, bf16[2,2,96,512]{3,2,0,1:T(8,128)(2,1)}, u32[]{:S(2)}, u32[]{:S(2)}) %collective-permute-start.1) | collective-permute-done | bytes 393248 | tf_op jit(solution)/shard_map/while/body/eval_jaxpr/ppermute | solution.py:27
  556.0 20.0 %collective-permute-done.1 = bf16[2,2,96,512]{3,2,0,1:T(8,128)(2,1)} collective-permute-done((bf16[2,2,96,512]{3,2,0,1:T(8,128)(2,1)}, bf16[2,2,96,512]{3,2,0,1:T(8,128)(2,1)}, u32[]{:S(2)}, u32[]{:S(2)}) %collective-permute-start.1) | collective-permute-done | bytes 393248 | tf_op jit(solution)/shard_map/while/body/eval_jaxpr/ppermute | solution.py:27
  578.1 10.3 %collective-permute-done.1 = bf16[2,2,96,512]{3,2,0,1:T(8,128)(2,1)} collective-permute-done((bf16[2,2,96,512]{3,2,0,1:T(8,128)(2,1)}, bf16[2,2,96,512]{3,2,0,1:T(8,128)(2,1)}, u32[]{:S(2)}, u32[]{:S(2)}) %collective-permute-start.1) | collective-permute-done | bytes 393248 | tf_op jit(solution)/shard_map/while/body/eval_jaxpr/ppermute | solution.py:27
  590.5 10.8 %collective-permute-done.1 = bf16[2,2,96,512]{3,2,0,1:T(8,128)(2,1)} collective-permute-done((bf16[2,2,96,512]{3,2,0,1:T(8,128)(2,1)}, bf16[2,2,96,512]{3,2,0,1:T(8,128)(2,1)}, u32[]{:S(2)}, u32[]{:S(2)}) %collective-permute-start.1) | collective-permute-done | bytes 393248 | tf_op jit(solution)/shard_map/while/body/eval_jaxpr/ppermute | solution.py:27
  603.3 192.9 %collective-permute-done.1 = bf16[2,2,96,512]{3,2,0,1:T(8,128)(2,1)} collective-permute-done((bf16[2,2,96,512]{3,2,0,1:T(8,128)(2,1)}, bf16[2,2,96,512]{3,2,0,1:T(8,128)(2,1)}, u32[]{:S(2)}, u32[]{:S(2)}) %collective-permute-start.1) | collective-permute-done | bytes 393248 | tf_op jit(solution)/shard_map/while/body/eval_jaxpr/ppermute | solution.py:27
  796.2 13.7 %conditional.5 = ((bf16[2,2,1,96,512]{4,3,1,2,0:T(8,128)(2,1)}, bf16[2,2,96,512]{3,2,1,0:T(8,128)(2,1)S(1)})) conditional(s32[]{:T(128)} %convert_element_type.124, (bf16[2,2,1,96,512]{4,3,1,2,0:T(8,128)(2,1)}, bf16[2,2,96,512]{3,2,1,0:T(8,128)(2,1)S(1)}) %tuple.91, (bf16[2,2,1,96,512]{4,3,1,2,0:T(8,128)(2,1)}, ...), branch_computations={%region_5.0_spmd, %region_6.0_spmd} | conditional | flops 806879232 | bytes 23461968 | solution.py:117
  801.6 2.0 reshape.124
  803.6 2.4 fusion.18
  806.1 2.0 reshape.123
  (118 shorter events, 76.2 us)
Async XLA Ops:
  0.0 28.2 %copy-start.6 = (f32[4]{0:T(128)S(1)}, f32[4]{0:T(128)}, u32[]{:S(2)}) copy-start(f32[4]{0:T(128)} %param.21) | copy-start | bytes 52
  0.0 29.4 %collective-permute-start.2 = (bf16[2,2,1,96,512]{4,3,1,0,2:T(8,128)(2,1)}, bf16[2,2,1,96,512]{4,3,1,0,2:T(8,128)(2,1)S(1)}, u32[]{:S(2)}, u32[]{:S(2)}) collective-permute-start(bf16[2,2,1,96,512]{4,3,1,0,2:T(8,128)(2,1)} %bitcast.112), channel_id=1, source_target_pairs={{0,1},{1,2},{2,3},{3,4},{4,5},{5,6},{6,7},{7,8},{8,9},{9,10},{10,1... | collective-permute-start | bytes 1179656 | tf_op jit(solution)/shard_map/ppermute | solution.py:15
  2.1 27.6 %collective-permute-start.3 = (bf16[2,2,1,96,512]{4,3,1,0,2:T(8,128)(2,1)}, bf16[2,2,1,96,512]{4,3,1,0,2:T(8,128)(2,1)S(1)}, u32[]{:S(2)}, u32[]{:S(2)}) collective-permute-start(bf16[2,2,1,96,512]{4,3,1,0,2:T(8,128)(2,1)} %bitcast.113), channel_id=1, source_target_pairs={{1,0},{2,1},{3,2},{4,3},{5,4},{6,5},{7,6},{8,7},{9,8},{10,9},{11,1... | collective-permute-start | bytes 1179656 | tf_op jit(solution)/shard_map/ppermute | solution.py:17
  26.7 3.0 copy-start.4
  28.9 1.0 copy-start.5
  29.9 4.9 copy-start
  36.5 9.1 %collective-permute-start = (bf16[2,2,96,512]{3,2,1,0:T(8,128)(2,1)}, bf16[2,2,96,512]{3,2,1,0:T(8,128)(2,1)}, u32[]{:S(2)}, u32[]{:S(2)}) collective-permute-start(bf16[2,2,96,512]{3,2,1,0:T(8,128)(2,1)} %copy.41), channel_id=1, source_target_pairs={{0,32},{32,64},{64,96},{96,128},{128,160},{160,192},{192,224},{224... | collective-permute-start | bytes 1179656 | tf_op jit(solution)/shard_map/while/body/eval_jaxpr/ppermute | solution.py:27
  53.4 1.6 copy-start.1
  59.8 6.9 collective-permute-start
  68.4 23.5 %collective-permute-start = (bf16[2,2,96,512]{3,2,1,0:T(8,128)(2,1)}, bf16[2,2,96,512]{3,2,1,0:T(8,128)(2,1)}, u32[]{:S(2)}, u32[]{:S(2)}) collective-permute-start(bf16[2,2,96,512]{3,2,1,0:T(8,128)(2,1)} %copy.41), channel_id=1, source_target_pairs={{0,32},{32,64},{64,96},{96,128},{128,160},{160,192},{192,224},{224... | collective-permute-start | bytes 1179656 | tf_op jit(solution)/shard_map/while/body/eval_jaxpr/ppermute | solution.py:27
  93.7 12.2 %collective-permute-start = (bf16[2,2,96,512]{3,2,1,0:T(8,128)(2,1)}, bf16[2,2,96,512]{3,2,1,0:T(8,128)(2,1)}, u32[]{:S(2)}, u32[]{:S(2)}) collective-permute-start(bf16[2,2,96,512]{3,2,1,0:T(8,128)(2,1)} %copy.41), channel_id=1, source_target_pairs={{0,32},{32,64},{64,96},{96,128},{128,160},{160,192},{192,224},{224... | collective-permute-start | bytes 1179656 | tf_op jit(solution)/shard_map/while/body/eval_jaxpr/ppermute | solution.py:27
  107.6 22.1 %collective-permute-start = (bf16[2,2,96,512]{3,2,1,0:T(8,128)(2,1)}, bf16[2,2,96,512]{3,2,1,0:T(8,128)(2,1)}, u32[]{:S(2)}, u32[]{:S(2)}) collective-permute-start(bf16[2,2,96,512]{3,2,1,0:T(8,128)(2,1)} %copy.41), channel_id=1, source_target_pairs={{0,32},{32,64},{64,96},{96,128},{128,160},{160,192},{192,224},{224... | collective-permute-start | bytes 1179656 | tf_op jit(solution)/shard_map/while/body/eval_jaxpr/ppermute | solution.py:27
  131.5 14.2 %collective-permute-start = (bf16[2,2,96,512]{3,2,1,0:T(8,128)(2,1)}, bf16[2,2,96,512]{3,2,1,0:T(8,128)(2,1)}, u32[]{:S(2)}, u32[]{:S(2)}) collective-permute-start(bf16[2,2,96,512]{3,2,1,0:T(8,128)(2,1)} %copy.41), channel_id=1, source_target_pairs={{0,32},{32,64},{64,96},{96,128},{128,160},{160,192},{192,224},{224... | collective-permute-start | bytes 1179656 | tf_op jit(solution)/shard_map/while/body/eval_jaxpr/ppermute | solution.py:27
  147.5 23.0 %collective-permute-start = (bf16[2,2,96,512]{3,2,1,0:T(8,128)(2,1)}, bf16[2,2,96,512]{3,2,1,0:T(8,128)(2,1)}, u32[]{:S(2)}, u32[]{:S(2)}) collective-permute-start(bf16[2,2,96,512]{3,2,1,0:T(8,128)(2,1)} %copy.41), channel_id=1, source_target_pairs={{0,32},{32,64},{64,96},{96,128},{128,160},{160,192},{192,224},{224... | collective-permute-start | bytes 1179656 | tf_op jit(solution)/shard_map/while/body/eval_jaxpr/ppermute | solution.py:27
  172.2 13.1 %collective-permute-start = (bf16[2,2,96,512]{3,2,1,0:T(8,128)(2,1)}, bf16[2,2,96,512]{3,2,1,0:T(8,128)(2,1)}, u32[]{:S(2)}, u32[]{:S(2)}) collective-permute-start(bf16[2,2,96,512]{3,2,1,0:T(8,128)(2,1)} %copy.41), channel_id=1, source_target_pairs={{0,32},{32,64},{64,96},{96,128},{128,160},{160,192},{192,224},{224... | collective-permute-start | bytes 1179656 | tf_op jit(solution)/shard_map/while/body/eval_jaxpr/ppermute | solution.py:27
  187.0 23.9 %collective-permute-start = (bf16[2,2,96,512]{3,2,1,0:T(8,128)(2,1)}, bf16[2,2,96,512]{3,2,1,0:T(8,128)(2,1)}, u32[]{:S(2)}, u32[]{:S(2)}) collective-permute-start(bf16[2,2,96,512]{3,2,1,0:T(8,128)(2,1)} %copy.41), channel_id=1, source_target_pairs={{0,32},{32,64},{64,96},{96,128},{128,160},{160,192},{192,224},{224... | collective-permute-start | bytes 1179656 | tf_op jit(solution)/shard_map/while/body/eval_jaxpr/ppermute | solution.py:27
  212.7 12.5 %collective-permute-start = (bf16[2,2,96,512]{3,2,1,0:T(8,128)(2,1)}, bf16[2,2,96,512]{3,2,1,0:T(8,128)(2,1)}, u32[]{:S(2)}, u32[]{:S(2)}) collective-permute-start(bf16[2,2,96,512]{3,2,1,0:T(8,128)(2,1)} %copy.41), channel_id=1, source_target_pairs={{0,32},{32,64},{64,96},{96,128},{128,160},{160,192},{192,224},{224... | collective-permute-start | bytes 1179656 | tf_op jit(solution)/shard_map/while/body/eval_jaxpr/ppermute | solution.py:27
  227.0 18.9 %collective-permute-start = (bf16[2,2,96,512]{3,2,1,0:T(8,128)(2,1)}, bf16[2,2,96,512]{3,2,1,0:T(8,128)(2,1)}, u32[]{:S(2)}, u32[]{:S(2)}) collective-permute-start(bf16[2,2,96,512]{3,2,1,0:T(8,128)(2,1)} %copy.41), channel_id=1, source_target_pairs={{0,32},{32,64},{64,96},{96,128},{128,160},{160,192},{192,224},{224... | collective-permute-start | bytes 1179656 | tf_op jit(solution)/shard_map/while/body/eval_jaxpr/ppermute | solution.py:27
  247.6 12.1 %collective-permute-start = (bf16[2,2,96,512]{3,2,1,0:T(8,128)(2,1)}, bf16[2,2,96,512]{3,2,1,0:T(8,128)(2,1)}, u32[]{:S(2)}, u32[]{:S(2)}) collective-permute-start(bf16[2,2,96,512]{3,2,1,0:T(8,128)(2,1)} %copy.41), channel_id=1, source_target_pairs={{0,32},{32,64},{64,96},{96,128},{128,160},{160,192},{192,224},{224... | collective-permute-start | bytes 1179656 | tf_op jit(solution)/shard_map/while/body/eval_jaxpr/ppermute | solution.py:27
  261.5 19.2 %collective-permute-start = (bf16[2,2,96,512]{3,2,1,0:T(8,128)(2,1)}, bf16[2,2,96,512]{3,2,1,0:T(8,128)(2,1)}, u32[]{:S(2)}, u32[]{:S(2)}) collective-permute-start(bf16[2,2,96,512]{3,2,1,0:T(8,128)(2,1)} %copy.41), channel_id=1, source_target_pairs={{0,32},{32,64},{64,96},{96,128},{128,160},{160,192},{192,224},{224... | collective-permute-start | bytes 1179656 | tf_op jit(solution)/shard_map/while/body/eval_jaxpr/ppermute | solution.py:27
  282.4 12.1 %collective-permute-start = (bf16[2,2,96,512]{3,2,1,0:T(8,128)(2,1)}, bf16[2,2,96,512]{3,2,1,0:T(8,128)(2,1)}, u32[]{:S(2)}, u32[]{:S(2)}) collective-permute-start(bf16[2,2,96,512]{3,2,1,0:T(8,128)(2,1)} %copy.41), channel_id=1, source_target_pairs={{0,32},{32,64},{64,96},{96,128},{128,160},{160,192},{192,224},{224... | collective-permute-start | bytes 1179656 | tf_op jit(solution)/shard_map/while/body/eval_jaxpr/ppermute | solution.py:27
  296.2 19.2 %collective-permute-start = (bf16[2,2,96,512]{3,2,1,0:T(8,128)(2,1)}, bf16[2,2,96,512]{3,2,1,0:T(8,128)(2,1)}, u32[]{:S(2)}, u32[]{:S(2)}) collective-permute-start(bf16[2,2,96,512]{3,2,1,0:T(8,128)(2,1)} %copy.41), channel_id=1, source_target_pairs={{0,32},{32,64},{64,96},{96,128},{128,160},{160,192},{192,224},{224... | collective-permute-start | bytes 1179656 | tf_op jit(solution)/shard_map/while/body/eval_jaxpr/ppermute | solution.py:27
  317.2 12.1 %collective-permute-start = (bf16[2,2,96,512]{3,2,1,0:T(8,128)(2,1)}, bf16[2,2,96,512]{3,2,1,0:T(8,128)(2,1)}, u32[]{:S(2)}, u32[]{:S(2)}) collective-permute-start(bf16[2,2,96,512]{3,2,1,0:T(8,128)(2,1)} %copy.41), channel_id=1, source_target_pairs={{0,32},{32,64},{64,96},{96,128},{128,160},{160,192},{192,224},{224... | collective-permute-start | bytes 1179656 | tf_op jit(solution)/shard_map/while/body/eval_jaxpr/ppermute | solution.py:27
  330.8 21.6 %collective-permute-start.1 = (bf16[2,2,96,512]{3,2,0,1:T(8,128)(2,1)}, bf16[2,2,96,512]{3,2,0,1:T(8,128)(2,1)}, u32[]{:S(2)}, u32[]{:S(2)}) collective-permute-start(bf16[2,2,96,512]{3,2,0,1:T(8,128)(2,1)} %copy.42), channel_id=1, source_target_pairs={{32,0},{64,32},{96,64},{128,96},{160,128},{192,160},{224,192},{256... | collective-permute-start | bytes 1179656 | tf_op jit(solution)/shard_map/while/body/eval_jaxpr/ppermute | solution.py:27
  353.2 12.6 %collective-permute-start.1 = (bf16[2,2,96,512]{3,2,0,1:T(8,128)(2,1)}, bf16[2,2,96,512]{3,2,0,1:T(8,128)(2,1)}, u32[]{:S(2)}, u32[]{:S(2)}) collective-permute-start(bf16[2,2,96,512]{3,2,0,1:T(8,128)(2,1)} %copy.42), channel_id=1, source_target_pairs={{32,0},{64,32},{96,64},{128,96},{160,128},{192,160},{224,192},{256... | collective-permute-start | bytes 1179656 | tf_op jit(solution)/shard_map/while/body/eval_jaxpr/ppermute | solution.py:27
  366.5 20.2 %collective-permute-start.1 = (bf16[2,2,96,512]{3,2,0,1:T(8,128)(2,1)}, bf16[2,2,96,512]{3,2,0,1:T(8,128)(2,1)}, u32[]{:S(2)}, u32[]{:S(2)}) collective-permute-start(bf16[2,2,96,512]{3,2,0,1:T(8,128)(2,1)} %copy.42), channel_id=1, source_target_pairs={{32,0},{64,32},{96,64},{128,96},{160,128},{192,160},{224,192},{256... | collective-permute-start | bytes 1179656 | tf_op jit(solution)/shard_map/while/body/eval_jaxpr/ppermute | solution.py:27
  387.5 11.4 %collective-permute-start.1 = (bf16[2,2,96,512]{3,2,0,1:T(8,128)(2,1)}, bf16[2,2,96,512]{3,2,0,1:T(8,128)(2,1)}, u32[]{:S(2)}, u32[]{:S(2)}) collective-permute-start(bf16[2,2,96,512]{3,2,0,1:T(8,128)(2,1)} %copy.42), channel_id=1, source_target_pairs={{32,0},{64,32},{96,64},{128,96},{160,128},{192,160},{224,192},{256... | collective-permute-start | bytes 1179656 | tf_op jit(solution)/shard_map/while/body/eval_jaxpr/ppermute | solution.py:27
  399.8 24.5 %collective-permute-start.1 = (bf16[2,2,96,512]{3,2,0,1:T(8,128)(2,1)}, bf16[2,2,96,512]{3,2,0,1:T(8,128)(2,1)}, u32[]{:S(2)}, u32[]{:S(2)}) collective-permute-start(bf16[2,2,96,512]{3,2,0,1:T(8,128)(2,1)} %copy.42), channel_id=1, source_target_pairs={{32,0},{64,32},{96,64},{128,96},{160,128},{192,160},{224,192},{256... | collective-permute-start | bytes 1179656 | tf_op jit(solution)/shard_map/while/body/eval_jaxpr/ppermute | solution.py:27
  425.0 10.0 %collective-permute-start.1 = (bf16[2,2,96,512]{3,2,0,1:T(8,128)(2,1)}, bf16[2,2,96,512]{3,2,0,1:T(8,128)(2,1)}, u32[]{:S(2)}, u32[]{:S(2)}) collective-permute-start(bf16[2,2,96,512]{3,2,0,1:T(8,128)(2,1)} %copy.42), channel_id=1, source_target_pairs={{32,0},{64,32},{96,64},{128,96},{160,128},{192,160},{224,192},{256... | collective-permute-start | bytes 1179656 | tf_op jit(solution)/shard_map/while/body/eval_jaxpr/ppermute | solution.py:27
  435.8 28.0 %collective-permute-start.1 = (bf16[2,2,96,512]{3,2,0,1:T(8,128)(2,1)}, bf16[2,2,96,512]{3,2,0,1:T(8,128)(2,1)}, u32[]{:S(2)}, u32[]{:S(2)}) collective-permute-start(bf16[2,2,96,512]{3,2,0,1:T(8,128)(2,1)} %copy.42), channel_id=1, source_target_pairs={{32,0},{64,32},{96,64},{128,96},{160,128},{192,160},{224,192},{256... | collective-permute-start | bytes 1179656 | tf_op jit(solution)/shard_map/while/body/eval_jaxpr/ppermute | solution.py:27
  464.6 13.4 %collective-permute-start.1 = (bf16[2,2,96,512]{3,2,0,1:T(8,128)(2,1)}, bf16[2,2,96,512]{3,2,0,1:T(8,128)(2,1)}, u32[]{:S(2)}, u32[]{:S(2)}) collective-permute-start(bf16[2,2,96,512]{3,2,0,1:T(8,128)(2,1)} %copy.42), channel_id=1, source_target_pairs={{32,0},{64,32},{96,64},{128,96},{160,128},{192,160},{224,192},{256... | collective-permute-start | bytes 1179656 | tf_op jit(solution)/shard_map/while/body/eval_jaxpr/ppermute | solution.py:27
  478.7 25.4 %collective-permute-start.1 = (bf16[2,2,96,512]{3,2,0,1:T(8,128)(2,1)}, bf16[2,2,96,512]{3,2,0,1:T(8,128)(2,1)}, u32[]{:S(2)}, u32[]{:S(2)}) collective-permute-start(bf16[2,2,96,512]{3,2,0,1:T(8,128)(2,1)} %copy.42), channel_id=1, source_target_pairs={{32,0},{64,32},{96,64},{128,96},{160,128},{192,160},{224,192},{256... | collective-permute-start | bytes 1179656 | tf_op jit(solution)/shard_map/while/body/eval_jaxpr/ppermute | solution.py:27
  504.8 14.8 %collective-permute-start.1 = (bf16[2,2,96,512]{3,2,0,1:T(8,128)(2,1)}, bf16[2,2,96,512]{3,2,0,1:T(8,128)(2,1)}, u32[]{:S(2)}, u32[]{:S(2)}) collective-permute-start(bf16[2,2,96,512]{3,2,0,1:T(8,128)(2,1)} %copy.42), channel_id=1, source_target_pairs={{32,0},{64,32},{96,64},{128,96},{160,128},{192,160},{224,192},{256... | collective-permute-start | bytes 1179656 | tf_op jit(solution)/shard_map/while/body/eval_jaxpr/ppermute | solution.py:27
  520.4 20.7 %collective-permute-start.1 = (bf16[2,2,96,512]{3,2,0,1:T(8,128)(2,1)}, bf16[2,2,96,512]{3,2,0,1:T(8,128)(2,1)}, u32[]{:S(2)}, u32[]{:S(2)}) collective-permute-start(bf16[2,2,96,512]{3,2,0,1:T(8,128)(2,1)} %copy.42), channel_id=1, source_target_pairs={{32,0},{64,32},{96,64},{128,96},{160,128},{192,160},{224,192},{256... | collective-permute-start | bytes 1179656 | tf_op jit(solution)/shard_map/while/body/eval_jaxpr/ppermute | solution.py:27
  541.8 12.1 %collective-permute-start.1 = (bf16[2,2,96,512]{3,2,0,1:T(8,128)(2,1)}, bf16[2,2,96,512]{3,2,0,1:T(8,128)(2,1)}, u32[]{:S(2)}, u32[]{:S(2)}) collective-permute-start(bf16[2,2,96,512]{3,2,0,1:T(8,128)(2,1)} %copy.42), channel_id=1, source_target_pairs={{32,0},{64,32},{96,64},{128,96},{160,128},{192,160},{224,192},{256... | collective-permute-start | bytes 1179656 | tf_op jit(solution)/shard_map/while/body/eval_jaxpr/ppermute | solution.py:27
  554.8 21.3 %collective-permute-start.1 = (bf16[2,2,96,512]{3,2,0,1:T(8,128)(2,1)}, bf16[2,2,96,512]{3,2,0,1:T(8,128)(2,1)}, u32[]{:S(2)}, u32[]{:S(2)}) collective-permute-start(bf16[2,2,96,512]{3,2,0,1:T(8,128)(2,1)} %copy.42), channel_id=1, source_target_pairs={{32,0},{64,32},{96,64},{128,96},{160,128},{192,160},{224,192},{256... | collective-permute-start | bytes 1179656 | tf_op jit(solution)/shard_map/while/body/eval_jaxpr/ppermute | solution.py:27
  576.8 11.6 %collective-permute-start.1 = (bf16[2,2,96,512]{3,2,0,1:T(8,128)(2,1)}, bf16[2,2,96,512]{3,2,0,1:T(8,128)(2,1)}, u32[]{:S(2)}, u32[]{:S(2)}) collective-permute-start(bf16[2,2,96,512]{3,2,0,1:T(8,128)(2,1)} %copy.42), channel_id=1, source_target_pairs={{32,0},{64,32},{96,64},{128,96},{160,128},{192,160},{224,192},{256... | collective-permute-start | bytes 1179656 | tf_op jit(solution)/shard_map/while/body/eval_jaxpr/ppermute | solution.py:27
  589.2 12.1 %collective-permute-start.1 = (bf16[2,2,96,512]{3,2,0,1:T(8,128)(2,1)}, bf16[2,2,96,512]{3,2,0,1:T(8,128)(2,1)}, u32[]{:S(2)}, u32[]{:S(2)}) collective-permute-start(bf16[2,2,96,512]{3,2,0,1:T(8,128)(2,1)} %copy.42), channel_id=1, source_target_pairs={{32,0},{64,32},{96,64},{128,96},{160,128},{192,160},{224,192},{256... | collective-permute-start | bytes 1179656 | tf_op jit(solution)/shard_map/while/body/eval_jaxpr/ppermute | solution.py:27
  602.0 194.2 %collective-permute-start.1 = (bf16[2,2,96,512]{3,2,0,1:T(8,128)(2,1)}, bf16[2,2,96,512]{3,2,0,1:T(8,128)(2,1)}, u32[]{:S(2)}, u32[]{:S(2)}) collective-permute-start(bf16[2,2,96,512]{3,2,0,1:T(8,128)(2,1)} %copy.42), channel_id=1, source_target_pairs={{32,0},{64,32},{96,64},{128,96},{160,128},{192,160},{224,192},{256... | collective-permute-start | bytes 1179656 | tf_op jit(solution)/shard_map/while/body/eval_jaxpr/ppermute | solution.py:27
  797.7 1.7 copy-start.3
  808.1 1.6 copy-start.2
where the time goes:
time: 813 us; the launch traced here: 810 us
  waiting for transfers between devices  532 us (65%)
  starting transfers between devices  191 us (23%)
  local copies, waits for them, and re-layouts  57.1 us (7%)
  matrix products  12.1 us (1%)
  between operations  10.2 us (1%)
    ppermute x32, waiting for transfers between devices, passed_along(): lax.ppermute(value, axis, [(source, source + steps) for source in range(l...  531 us
    ppermute x32, starting transfers between devices, passed_along(): lax.ppermute(value, axis, [(source, source + steps) for source in range(l...  176 us
    another operation x32, local copies, waits for them, and re-layouts  40.4 us
  transfers between devices with their start and end apart: 34, of which 33 were waited for; matrix products, arithmetic and copies ran while one was open for 1% of the time, Pallas kernels for 0%

commit v1 on v0

v1 whole, which is shorter than its diff:
```python
import functools

import jax
import jax.numpy as jnp
from jax import lax
from jax.experimental import pallas as pl
from jax.experimental.pallas import tpu as pltpu
from jax.sharding import PartitionSpec as P

MESH = pl.DeviceIdType.MESH
F32 = jnp.float32
BF16 = jnp.bfloat16
ROWS = 16
SPAN = 4


def combined(product):
    h, w = product.shape[0] // 2, product.shape[1] // 2
    real = product[:h, :w] - product[h:, w:]
    imag = product[:h, w:] + product[h:, :w]
    return real, imag


def sweep_kernel(
    cuts, energies, inv_ref, cpl_ref, pat_ref, src_ref, prev_ref, off_ref, str_ref, out_ref,
    inv_v, it_v, cpl_v, cm_v, cmt_v, cm1_v, wf_v, we_v, src_v, prev_v, hl_v, hr_v,
    x_v, fin_v, u_v, bin_v,
    load_sem, hs_l, hs_r, hr_l, hr_r, cm_s, cm_r, wf_s, wf_r, we_s, we_r, a_s, a_r,
    f_s, f_r, b_s, b_r, o_s, o_r, turn_sem,
):
    blocks = pat_ref.shape[-1]
    no = inv_v.shape[-1]
    half = no // 2
    nb = no // blocks
    row_blocks = src_v.shape[2] // ROWS
    chunks = 4 * row_blocks
    pos = lax.axis_index("cuts")
    e = lax.axis_index("energy")
    core = lax.rem(e, 2)
    last = cuts - 1

    def rows(rb):
        return pl.ds(pl.multiple_of(rb * ROWS, ROWS), ROWS)

    def remote(src, dst, send, recv, device):
        return pltpu.make_async_remote_copy(
            src_ref=src, dst_ref=dst, send_sem=send, recv_sem=recv,
            device_id=device, device_id_type=MESH,
        )

    load_cpl = pltpu.make_async_copy(cpl_ref.at[:, 0], cpl_v, load_sem.at[0])
    load_inv = [
        pltpu.make_async_copy(inv_ref.at[:, l, 0], inv_v.at[l], load_sem.at[1 + l]) for l in range(2)
    ]
    load_src = pltpu.make_async_copy(src_ref.at[:, :, 0], src_v, load_sem.at[3])
    load_prev = pltpu.make_async_copy(prev_ref.at[:, :, 0], prev_v, load_sem.at[4])
    load_cpl.start()
    for copy in load_inv:
        copy.start()
    load_src.start()
    load_prev.start()

    barrier = pltpu.get_barrier_semaphore()
    partners = (
        (pos > 0, {"cuts": pos - 1}),
        (pos < last, {"cuts": pos + 1}),
        (e > 0, {"energy": e - 1}),
        (e < energies - 1, {"energy": e + 1}),
        (pos >= SPAN, {"cuts": pos - SPAN}),
        (pos < cuts - SPAN, {"cuts": pos + SPAN}),
    )
    for there, device in partners:
        @pl.when(there)
        def _():
            pl.semaphore_signal(barrier, inc=1, device_id=device, device_id_type=MESH)
    pl.semaphore_wait(barrier, sum(jnp.where(there, 1, 0) for there, _ in partners))

    def halo_right(rb):
        return remote(prev_ref.at[:, :, 0, rows(rb)], hl_v.at[:, :, rows(rb)], hs_r.at[rb], hr_l.at[rb], {"energy": e + 1})

    def halo_left(rb):
        return remote(prev_ref.at[:, :, 0, rows(rb)], hr_v.at[:, :, rows(rb)], hs_l.at[rb], hr_r.at[rb], {"energy": e - 1})

    def start_halo():
        @pl.loop(0, row_blocks)
        def _(rb):
            @pl.when(e < energies - 1)
            def _():
                halo_right(rb).start()

            @pl.when(e > 0)
            def _():
                halo_left(rb).start()

    @pl.when(e == 0)
    def _():
        hl_v[...] = jnp.zeros(hl_v.shape, BF16)

    @pl.when(e == energies - 1)
    def _():
        hr_v[...] = jnp.zeros(hr_v.shape, BF16)

    @pl.when(pos < SPAN)
    def _():
        start_halo()

    load_cpl.wait()
    for a in range(blocks):
        for b in range(blocks):
            keep = pat_ref[0, a, b].astype(F32)
            t, top = divmod(a * nb, half)
            lanes = slice(b * nb, (b + 1) * nb)
            real = cpl_v[0, a * nb:(a + 1) * nb, lanes].astype(F32)
            imag = cpl_v[1, a * nb:(a + 1) * nb, lanes].astype(F32)
            cm_v[t, top:top + nb, lanes] = (real * (-keep)).astype(BF16)
            cm_v[t, half + top:half + top + nb, lanes] = (imag * keep).astype(BF16)
    send_cm = remote(cm_v, cm1_v, cm_s, cm_r, {"cuts": pos - 1})

    @pl.when(lax.rem(pos, SPAN) != 0)
    def _():
        send_cm.start()

    for l in range(2):
        load_inv[l].wait()
        it_v[l, :, :no] = inv_v[l, 0].T
        it_v[l, :, no:] = inv_v[l, 1].T

    def product_into(left, right_l, target, slot):
        @pl.loop(0, 2)
        def _(t):
            product = jnp.dot(left[t], it_v[right_l], preferred_element_type=F32)
            real, imag = combined(product)
            top = pl.ds(pl.multiple_of(t * half, half), half)
            target[slot, top, :no] = real.astype(BF16)
            target[slot, top, no:] = imag.astype(BF16)

    def to_mate(ref, slot, send, recv):
        return remote(ref.at[slot], ref.at[slot], send, recv, {"energy": e + 1})

    @pl.when(pos > 0)
    def _():
        for t in range(2):
            lanes = slice(t * half, (t + 1) * half)
            real = cm_v[t, :half, :].T
            imag = -(cm_v[t, half:, :].T)
            for s in range(2):
                cmt_v[s, :half, lanes] = real[s * half:(s + 1) * half]
                cmt_v[s, half:, lanes] = imag[s * half:(s + 1) * half]

        @pl.loop(0, 2)
        def _(l):
            product_into(cmt_v, l, wf_v, 2 * core + l)

            @pl.when(core == 0)
            def _():
                to_mate(wf_v, l, wf_s.at[l], wf_r.at[l]).start()

    @pl.when(pos >= SPAN)
    def _():
        pl.semaphore_wait(turn_sem, 1)
        start_halo()

    @pl.when((pos > 0) & (lax.rem(pos, SPAN) == 0))
    def _():
        send_cm.start()

    near = F32(0)
    far = F32(0)
    for mode in range(off_ref.shape[0]):
        near = near + jnp.where(off_ref[mode] == 1, str_ref[mode], F32(0))
        far = far + jnp.where(off_ref[mode] == 2, str_ref[mode], F32(0))
    load_src.wait()
    load_prev.wait()

    def send_forward(n):
        return remote(x_v.at[n], fin_v.at[n], f_s.at[n], f_r.at[n], {"cuts": pos + 1})

    def send_backward(ref, n):
        return remote(ref.at[n], bin_v.at[n], b_s.at[n], b_r.at[n], {"cuts": pos - 1})

    def send_a(rb, l):
        return remote(x_v.at[4 * rb + l], x_v.at[4 * rb + l], a_s.at[2 * rb + l], a_r.at[2 * rb + l], {"energy": e + 1})

    @pl.loop(0, row_blocks)
    def _(rb):
        at = rows(rb)

        @pl.when(e > 0)
        def _():
            halo_right(rb).wait_recv()

        @pl.when(e < energies - 1)
        def _():
            halo_left(rb).wait_recv()

        @pl.when((rb == 1) & (pos < cuts - SPAN))
        def _():
            pl.semaphore_signal(turn_sem, inc=1, device_id={"cuts": pos + SPAN}, device_id_type=MESH)

        own = [prev_v[:, l, at, :].astype(F32) for l in range(2)]
        lo = [hl_v[:, l, at, :].astype(F32) for l in range(2)]
        hi = [hr_v[:, l, at, :].astype(F32) for l in range(2)]
        drives = (
            src_v[:, 0, at, :].astype(F32) + near * (own[1] + lo[1]) + far * (hi[0] + lo[0]),
            src_v[:, 1, at, :].astype(F32) + near * (hi[0] + own[0]) + far * (hi[1] + lo[1]),
        )
        for l in range(2):
            left = drives[l].astype(BF16).reshape(2 * ROWS, no)
            real, imag = combined(jnp.dot(left, it_v[l], preferred_element_type=F32))
            n = 4 * rb + 2 * core + l
            x_v[n, 0] = real.astype(BF16)
            x_v[n, 1] = imag.astype(BF16)

            @pl.when(core == 0)
            def _():
                send_a(rb, l).start()

            @pl.when((core == 1) & (pos == 0))
            def _():
                send_forward(n).start()

        @pl.when((core == 1) & (pos == 0))
        def _():
            for l in range(2):
                send_a(rb, l).wait_recv()
                send_forward(4 * rb + l).start()

    def own_we():
        remote(cm_v, cm1_v, cm_s, cm_r, {"cuts": pos - 1}).wait_recv()

        @pl.loop(0, 2)
        def _(l):
            product_into(cm1_v, l, we_v, 2 * core + l)

            @pl.when(core == 0)
            def _():
                to_mate(we_v, l, we_s.at[l], we_r.at[l]).start()

    def out_mate(ref, n):
        rb, slot = lax.div(n, 4), lax.rem(n, 4)
        return remote(
            ref.at[n], out_ref.at[:, slot, 0, rows(rb)], o_s.at[n], o_r.at[2 * rb + slot], {"energy": e - 1}
        )

    def out_own(ref, n):
        rb, slot = lax.div(n, 4), lax.rem(n, 4)
        return pltpu.make_async_copy(ref.at[n], out_ref.at[:, slot - 2, 0, rows(rb)], o_s.at[n])

    def write_out(ref, n):
        @pl.when(lax.rem(n, 4) < 2)
        def _():
            out_mate(ref, n).start()

        @pl.when(lax.rem(n, 4) >= 2)
        def _():
            out_own(ref, n).start()

    def stepped(given, weights, added, n):
        left = given[n].reshape(2 * ROWS, no)
        real, imag = combined(jnp.dot(left, weights[lax.rem(n, 4)], preferred_element_type=F32))
        return (real + added[n, 0].astype(F32)).astype(BF16), (imag + added[n, 1].astype(F32)).astype(BF16)

    def forward_step(n):
        @pl.when(n < 2)
        def _():
            to_mate(wf_v, n, wf_s.at[n], wf_r.at[n]).wait_recv()

        @pl.when(lax.rem(n, 4) < 2)
        def _():
            send_a(lax.div(n, 4), lax.rem(n, 4)).wait_recv()

        send_forward(n).wait_recv()
        x_v[n, 0], x_v[n, 1] = stepped(fin_v, wf_v, x_v, n)

        @pl.when(pos < last)
        def _():
            send_forward(n).start()

        @pl.when(pos == last)
        def _():
            send_backward(x_v, n).start()
            write_out(x_v, n)

    def backward_step(n):
        @pl.when(n < 2)
        def _():
            to_mate(we_v, n, we_s.at[n], we_r.at[n]).wait_recv()

        send_backward(u_v, n).wait_recv()
        u_v[n, 0], u_v[n, 1] = stepped(bin_v, we_v, x_v, n)

        @pl.when(pos > 0)
        def _():
            send_backward(u_v, n).start()

        write_out(u_v, n)

    lag = jnp.minimum(7 * (last - pos), chunks)

    def tick(n, _):
        @pl.when((n < chunks) & (pos > 0))
        def _():
            forward_step(n)

        @pl.when((n >= lag) & (pos < last))
        def _():
            backward_step(n - lag)

        return 0

    split = jnp.where(lag < chunks, 0, chunks)

    @pl.when(core == 1)
    def _():
        lax.fori_loop(0, split, tick, 0)

    @pl.when(pos < last)
    def _():
        own_we()

    @pl.when(core == 1)
    def _():
        lax.fori_loop(split, chunks + lag, tick, 0)

    @pl.when(core == 0)
    def _():
        @pl.loop(0, row_blocks)
        def _(rb):
            for l in range(2):
                remote(
                    u_v.at[4 * rb + l], out_ref.at[:, l, 0, rows(rb)], o_s.at[4 * rb + l], o_r.at[2 * rb + l],
                    {"energy": e + 1},
                ).wait_recv()
                send_a(rb, l).wait_send()

        for l in range(2):
            @pl.when(pos > 0)
            def _():
                to_mate(wf_v, l, wf_s.at[l], wf_r.at[l]).wait_send()

            @pl.when(pos < last)
            def _():
                to_mate(we_v, l, we_s.at[l], we_r.at[l]).wait_send()

    @pl.when(core == 1)
    def _():
        @pl.loop(0, chunks)
        def _(n):
            @pl.when(pos < last)
            def _():
                send_forward(n).wait_send()

            @pl.when(pos > 0)
            def _():
                send_backward(u_v, n).wait_send()

            @pl.when(lax.rem(n, 4) < 2)
            def _():
                out_mate(u_v, n).wait_send()

            @pl.when(lax.rem(n, 4) >= 2)
            def _():
                out_own(u_v, n).wait()

    @pl.loop(0, row_blocks)
    def _(rb):
        @pl.when(e < energies - 1)
        def _():
            halo_right(rb).wait_send()

        @pl.when(e > 0)
        def _():
            halo_left(rb).wait_send()

    @pl.when(pos > 0)
    def _():
        send_cm.wait_send()


def on_device(cuts, energies, inverse, coupling, pattern, source, previous, offsets, strength):
    no, nr = source.shape[4], source.shape[3]
    row_blocks = nr // ROWS
    chunks = 4 * row_blocks
    dma = pltpu.SemaphoreType.DMA
    panel = pltpu.VMEM((2, 2, nr, no), BF16)
    pieces = pltpu.VMEM((chunks, 2, ROWS, no), BF16)
    stack = pltpu.VMEM((2, no, no), BF16)
    anywhere = pl.BlockSpec(memory_space=pl.ANY)
    scalars = pl.BlockSpec(memory_space=pltpu.SMEM)
    return pl.pallas_call(
        functools.partial(sweep_kernel, cuts, energies),
        name="sweeps",
        out_shape=jax.ShapeDtypeStruct(source.shape, BF16),
        in_specs=[anywhere, anywhere, scalars, anywhere, anywhere, scalars, scalars],
        out_specs=anywhere,
        scratch_shapes=[
            pltpu.VMEM((2, 2, no, no), BF16),
            pltpu.VMEM((2, no, 2 * no), BF16),
            stack, stack, stack, stack,
            pltpu.VMEM((4, no, 2 * no), BF16),
            pltpu.VMEM((4, no, 2 * no), BF16),
            panel, panel, panel, panel,
            pieces, pieces, pieces, pieces,
            dma((5,)),
            dma((row_blocks,)), dma((row_blocks,)), dma((row_blocks,)), dma((row_blocks,)),
            dma, dma,
            dma((2,)), dma((2,)), dma((2,)), dma((2,)),
            dma((2 * row_blocks,)), dma((2 * row_blocks,)),
            dma((chunks,)), dma((chunks,)), dma((chunks,)), dma((chunks,)),
            dma((chunks,)), dma((2 * row_blocks,)),
            pltpu.SemaphoreType.REGULAR,
        ],
        compiler_params=pltpu.CompilerParams(
            collective_id=0, has_side_effects=True, vmem_limit_bytes=48 << 20
        ),
    )(inverse, coupling, pattern, source, previous, offsets, strength)


def solution(mesh):
    return jax.shard_map(
        functools.partial(on_device, mesh.shape["cuts"], mesh.shape["energy"]),
        mesh=mesh,
        in_specs=(
            P(None, "energy", "cuts", None, None),
            P(None, "cuts", None, None),
            P("cuts", None, None),
            P(None, "energy", "cuts", None, None),
            P(None, "energy", "cuts", None, None),
            P(),
            P(),
        ),
        out_specs=P(None, "energy", "cuts", None, None),
        check_vma=False,
    )
```

time: 813 us -> 128 us (0.16)
  the two profiles are of different devices: /device:TPU:6 before, /device:TPU:1 now
where the time goes in v1:
time: 128 us; the launch traced here: 127 us
  Pallas kernels  120 us (94%)
  local copies, waits for them, and re-layouts  7.54 us (6%)
    pallas_call x1, Pallas kernels, on_device(): pl.pallas_call(functools.partial(sweep_kernel, cuts, energies), name='swe...  120 us
    unnamed x15, local copies, waits for them, and re-layouts  7.54 us

profile of v1, /device:TPU:1, one launch (start us, length us, event | category | flops | bytes accessed | tf_op | source)
XLA Modules:
  0.0 127.4 jit_solution(16753828739563608376)
XLA Ops:
  0.0 0.0 copy-start
  0.0 1.6 %copy-done = bf16[2,2,1,512,512]{4,3,2,1,0:T(8,128)(2,1)S(1)} copy-done((bf16[2,2,1,512,512]{4,3,2,1,0:T(8,128)(2,1)S(1)}, bf16[2,2,1,512,512]{4,3,2,1,0:T(8,128)(2,1)}, u32[]{:S(2)}) %copy-start) | copy-done | bytes 2097176
  1.6 0.0 copy-start.1
  1.6 1.2 copy-done.1
  2.8 0.0 copy-start.2
  2.8 1.0 copy-done.2
  3.8 0.0 copy-start.3
  3.8 1.0 copy-done.3
  4.8 0.0 copy-start.4
  4.8 0.7 copy-done.4
  5.5 0.0 copy-start.5
  5.5 0.7 copy-done.5
  6.1 0.0 copy-start.6
  6.2 0.7 copy-done.6
  6.8 119.8 %sweeps.1 = bf16[2,2,1,96,512]{4,3,2,1,0:T(8,128)(2,1)S(1)} custom-call(bf16[2,2,1,512,512]{4,3,2,1,0:T(8,128)(2,1)S(1)} %copy-done, bf16[2,1,512,512]{3,2,1,0:T(8,128)(2,1)S(1)} %copy-done.1, s32[1,4,4]{2,1,0:T(4,128)S(1)} %copy-done.4, bf16[2,2,1,96,512]{4,3,2,1,0:T(8,128)(2,1)S(1)} %copy-done.2, bf16[2,2,1,96,512]{4,3,2,1,0:T(8,128)(2,1)S(1)} %copy-done.3, ...), custom_call_target="tpu_custom_call" | custom-call | tf_op jit(solution)/shard_map/sweeps/pallas_call | solution.py:390
  126.6 0.7 copy.9
Async XLA Ops:
  0.0 1.6 %copy-start = (bf16[2,2,1,512,512]{4,3,2,1,0:T(8,128)(2,1)S(1)}, bf16[2,2,1,512,512]{4,3,2,1,0:T(8,128)(2,1)}, u32[]{:S(2)}) copy-start(bf16[2,2,1,512,512]{4,3,2,1,0:T(8,128)(2,1)} %inv_ref.1) | copy-start | bytes 6291460
  1.6 1.2 copy-start.1
  2.8 1.0 copy-start.2
  3.8 1.0 copy-start.3
  4.8 0.7 copy-start.4
  5.5 0.7 copy-start.5
  6.1 0.7 copy-start.6

commit v2 on v0

v2 whole, which is shorter than its diff:
```python
import functools

import jax
import jax.numpy as jnp
from jax import lax
from jax.experimental import pallas as pl
from jax.experimental.pallas import tpu as pltpu
from jax.sharding import PartitionSpec as P

MESH = pl.DeviceIdType.MESH
F32 = jnp.float32
BF16 = jnp.bfloat16
SPAN = 4
PARTS = 2


def combined(product):
    h, w = product.shape[0] // 2, product.shape[1] // 2
    real = product[:h, :w] - product[h:, w:]
    imag = product[:h, w:] + product[h:, :w]
    return real, imag


def sweep_kernel(
    cuts, energies, inv_ref, cpl_ref, pat_ref, src_ref, prev_ref, off_ref, str_ref, out_ref,
    inv_v, it_v, cpl_v, cm_v, cmt_v, cm1_v, wfo_v, weo_v, wf_v, we_v, src_v, prev_v, hl_v, hr_v,
    ao_v, x_v, u_v,
    load_sem, hs_l, hs_r, hr_l, hr_r, cm_s, cm_r, cx_s, cx_r, wf_s, wf_r, we_s, we_r, a_s, a_r,
    f_s, f_r, b_s, b_r, o_s, o_r,
):
    blocks = pat_ref.shape[-1]
    no = inv_v.shape[-1]
    nb = no // blocks
    width = src_v.shape[2] // PARTS
    pos = lax.axis_index("cuts")
    e = lax.axis_index("energy")
    core = lax.rem(e, 2)
    first_e = e - core
    last = cuts - 1
    place = lax.rem(pos, SPAN)
    base = pos - place
    xs = energies // SPAN
    stride = xs
    x = lax.div(e, stride)

    def rows(c):
        return pl.ds(c * width, width)

    def remote(src, dst, send, recv, device):
        return pltpu.make_async_remote_copy(
            src_ref=src, dst_ref=dst, send_sem=send, recv_sem=recv,
            device_id=device, device_id_type=MESH,
        )

    load_cpl = pltpu.make_async_copy(cpl_ref.at[:, 0], cpl_v, load_sem.at[0])
    load_inv = [
        pltpu.make_async_copy(inv_ref.at[:, l, 0], inv_v.at[l], load_sem.at[1 + l]) for l in range(2)
    ]
    load_src = pltpu.make_async_copy(src_ref.at[:, :, 0], src_v, load_sem.at[3])
    load_prev = pltpu.make_async_copy(prev_ref.at[:, :, 0], prev_v, load_sem.at[4])
    load_cpl.start()
    for copy in load_inv:
        copy.start()
    load_src.start()
    load_prev.start()

    def x_peer(step):
        return {"energy": lax.rem(x + step, SPAN) * stride + lax.rem(e, stride)}

    barrier = pltpu.get_barrier_semaphore()
    always = pos >= 0
    partners = [(always, {"energy": first_e + 1 - core})]
    for step in range(1, SPAN):
        there = base + lax.rem(place + step, SPAN)
        partners.append((always, {"cuts": there, "energy": first_e}))
        partners.append((always, {"cuts": there, "energy": first_e + 1}))
        partners.append((always, x_peer(step)))
    partners += [
        ((place == 0) & (pos > 0), {"cuts": pos - 1}),
        ((place == SPAN - 1) & (pos < last), {"cuts": pos + 1}),
        (pos >= SPAN, {"cuts": pos - SPAN}),
        (pos < cuts - SPAN, {"cuts": pos + SPAN}),
        ((core == 0) & (e > 0), {"energy": e - 1}),
        ((core == 1) & (e < energies - 1), {"energy": e + 1}),
    ]
    for there, device in partners:
        @pl.when(there)
        def _():
            pl.semaphore_signal(barrier, inc=1, device_id=device, device_id_type=MESH)
    pl.semaphore_wait(barrier, sum(jnp.where(there, 1, 0) for there, _ in partners))

    def halo_right(c):
        return remote(prev_ref.at[:, :, 0, rows(c)], hl_v.at[:, :, rows(c)], hs_r.at[c], hr_l.at[c], {"energy": e + 1})

    def halo_left(c):
        return remote(prev_ref.at[:, :, 0, rows(c)], hr_v.at[:, :, rows(c)], hs_l.at[c], hr_r.at[c], {"energy": e - 1})

    for c in range(PARTS):
        @pl.when(e < energies - 1)
        def _():
            halo_right(c).start()

        @pl.when(e > 0)
        def _():
            halo_left(c).start()

    load_cpl.wait()
    for a in range(blocks):
        for b in range(blocks):
            keep = pat_ref[0, a, b].astype(F32)
            lanes = slice(b * nb, (b + 1) * nb)
            real = cpl_v[0, a * nb:(a + 1) * nb, lanes].astype(F32)
            imag = cpl_v[1, a * nb:(a + 1) * nb, lanes].astype(F32)
            cm_v[a, :nb, lanes] = (real * (-keep)).astype(BF16)
            cm_v[a, nb:, lanes] = (imag * keep).astype(BF16)

    send_cm = remote(cm_v.at[x], cm1_v.at[x], cm_s, cm_r, {"cuts": pos - 1})

    def share_cm(step):
        return remote(cm1_v.at[x], cm1_v.at[x], cx_s.at[step - 1], cx_r.at[step - 1], x_peer(step))

    def shared_cm(step):
        slot = lax.rem(x + SPAN - step, SPAN)
        return remote(cm1_v.at[slot], cm1_v.at[slot], cx_s.at[step - 1], cx_r.at[step - 1], x_peer(step))

    @pl.when(pos > 0)
    def _():
        send_cm.start()

    for l in range(2):
        load_inv[l].wait()
        it_v[l, :, :no] = inv_v[l, 0].T
        it_v[l, :, no:] = inv_v[l, 1].T

    def product_into(left, l, target):
        @pl.loop(0, blocks)
        def _(t):
            product = jnp.dot(left[t], it_v[l], preferred_element_type=F32)
            real, imag = combined(product)
            top = pl.ds(pl.multiple_of(t * nb, nb), nb)
            target[l, top, :no] = real.astype(BF16)
            target[l, top, no:] = imag.astype(BF16)

    def owner(l):
        return {"cuts": base + 2 * core + l, "energy": first_e + 1}

    def is_owner(l):
        return (core == 1) & (place == 2 + l)

    def hand(src, dst, l, send, recv):
        @pl.when(is_owner(l))
        def _():
            pltpu.make_async_copy(src, dst, recv).start()

        @pl.when(jnp.logical_not(is_owner(l)))
        def _():
            remote(src, dst, send, recv, owner(l)).start()

    def handed(src, dst, l, send, recv):
        @pl.when(jnp.logical_not(is_owner(l)))
        def _():
            remote(src, dst, send, recv, owner(l)).wait_send()

    def wf_args(l):
        return wfo_v.at[l], wf_v.at[place], l, wf_s.at[l], wf_r.at[place]

    def we_args(l):
        return weo_v.at[l], we_v.at[place], l, we_s.at[l], we_r.at[place]

    def a_args(c, l):
        return ao_v.at[c, l], x_v.at[c, 1 + place], l, a_s.at[2 * c + l], a_r.at[PARTS * place + c]

    @pl.when(pos > 0)
    def _():
        for t in range(blocks):
            lanes = slice(t * nb, (t + 1) * nb)
            real = cm_v[t, :nb, :].T
            imag = -(cm_v[t, nb:, :].T)
            for s in range(blocks):
                cmt_v[s, :nb, lanes] = real[s * nb:(s + 1) * nb]
                cmt_v[s, nb:, lanes] = imag[s * nb:(s + 1) * nb]

        @pl.loop(0, 2)
        def _(l):
            product_into(cmt_v, l, wfo_v)
            hand(*wf_args(l))

    @pl.when(pos < last)
    def _():
        send_cm.wait_recv()
        for step in range(1, SPAN):
            share_cm(step).start()

    near = F32(0)
    far = F32(0)
    for mode in range(off_ref.shape[0]):
        near = near + jnp.where(off_ref[mode] == 1, str_ref[mode], F32(0))
        far = far + jnp.where(off_ref[mode] == 2, str_ref[mode], F32(0))
    load_src.wait()
    load_prev.wait()

    @pl.when(e == 0)
    def _():
        hl_v[...] = jnp.zeros(hl_v.shape, BF16)

    @pl.when(e == energies - 1)
    def _():
        hr_v[...] = jnp.zeros(hr_v.shape, BF16)

    for c in range(PARTS):
        at = rows(c)

        @pl.when(e > 0)
        def _():
            halo_right(c).wait_recv()

        @pl.when(e < energies - 1)
        def _():
            halo_left(c).wait_recv()

        own = [prev_v[:, l, at, :].astype(F32) for l in range(2)]
        lo = [hl_v[:, l, at, :].astype(F32) for l in range(2)]
        hi = [hr_v[:, l, at, :].astype(F32) for l in range(2)]
        drives = (
            src_v[:, 0, at, :].astype(F32) + near * (own[1] + lo[1]) + far * (hi[0] + lo[0]),
            src_v[:, 1, at, :].astype(F32) + near * (hi[0] + own[0]) + far * (hi[1] + lo[1]),
        )
        for l in range(2):
            left = drives[l].astype(BF16).reshape(2 * width, no)
            real, imag = combined(jnp.dot(left, it_v[l], preferred_element_type=F32))
            ao_v[c, l, 0] = real.astype(BF16)
            ao_v[c, l, 1] = imag.astype(BF16)
            hand(*a_args(c, l))

    @pl.when(pos < last)
    def _():
        for step in range(1, SPAN):
            shared_cm(step).wait_recv()

        @pl.loop(0, 2)
        def _(l):
            product_into(cm1_v, l, weo_v)

    @pl.when(pos > 0)
    def _():
        for l in range(2):
            handed(*wf_args(l))

    @pl.when(pos < last)
    def _():
        for l in range(2):
            hand(*we_args(l))

    def stepped(given, weights, added):
        left = given[...].reshape(2 * width, no)
        real, imag = combined(jnp.dot(left, weights[...], preferred_element_type=F32))
        return (real + added[0].astype(F32)).astype(BF16), (imag + added[1].astype(F32)).astype(BF16)

    def send_forward(c):
        return remote(x_v.at[c, SPAN], x_v.at[c, 0], f_s.at[c], f_r.at[c], {"cuts": pos + SPAN})

    def send_backward(c):
        return remote(u_v.at[c, 0], u_v.at[c, SPAN], b_s.at[c], b_r.at[c], {"cuts": pos - SPAN})

    def out_at(c, l):
        return out_ref.at[:, l, 0, rows(c)]

    def is_home(j):
        return (place >= 2) & (j == place)

    def out_far(c, j, l):
        device = {"cuts": base + j, "energy": first_e + lax.div(place, 2)}
        return remote(u_v.at[c, j], out_at(c, l), o_s.at[SPAN * c + j], o_r.at[2 * c + l], device)

    def out_here(c, j, l):
        return pltpu.make_async_copy(u_v.at[c, j], out_at(c, l), o_r.at[2 * c + l])

    half_place = lax.rem(place, 2)

    @pl.when(core == 1)
    def _():
        for c in range(PARTS):
            @pl.loop(0, SPAN)
            def _(j):
                remote(ao_v.at[c, 0], x_v.at[c, 1 + j], a_s.at[0], a_r.at[PARTS * j + c], owner(0)).wait_recv()

                @pl.when((j == 0) & (base > 0))
                def _():
                    send_forward(c).wait_recv()

                @pl.when(base + j > 0)
                def _():
                    if c == 0:
                        remote(wfo_v.at[0], wf_v.at[j], wf_s.at[0], wf_r.at[j], owner(0)).wait_recv()
                    here = x_v.at[c, 1 + j]
                    here[0], here[1] = stepped(x_v.at[c, j], wf_v.at[j], here)

            @pl.when(base < cuts - SPAN)
            def _():
                send_forward(c).start()

        for c in range(PARTS):
            @pl.loop(0, SPAN)
            def _(back):
                j = SPAN - 1 - back

                @pl.when((back == 0) & (base < cuts - SPAN))
                def _():
                    send_backward(c).wait_recv()

                @pl.when(base + j < last)
                def _():
                    if c == 0:
                        remote(weo_v.at[0], we_v.at[j], we_s.at[0], we_r.at[j], owner(0)).wait_recv()
                    here = u_v.at[c, j]
                    here[0], here[1] = stepped(u_v.at[c, j + 1], we_v.at[j], x_v.at[c, 1 + j])

                @pl.when(base + j == last)
                def _():
                    u_v[c, j] = x_v[c, 1 + j]

                @pl.when((j == 0) & (base > 0))
                def _():
                    send_backward(c).start()

                for l in range(2):
                    @pl.when((half_place == l) & is_home(j))
                    def _():
                        out_here(c, j, l).start()

                    @pl.when((half_place == l) & jnp.logical_not(is_home(j)))
                    def _():
                        out_far(c, j, l).start()

    for c in range(PARTS):
        for l in range(2):
            out_far(c, 0, l).wait_recv()
            handed(*a_args(c, l))

        @pl.when(core == 1)
        def _():
            @pl.loop(0, SPAN)
            def _(j):
                @pl.when(jnp.logical_not(is_home(j)))
                def _():
                    out_far(c, j, 0).wait_send()

            @pl.when(base < cuts - SPAN)
            def _():
                send_forward(c).wait_send()

            @pl.when(base > 0)
            def _():
                send_backward(c).wait_send()

        @pl.when(e < energies - 1)
        def _():
            halo_right(c).wait_send()

        @pl.when(e > 0)
        def _():
            halo_left(c).wait_send()

    @pl.when(pos > 0)
    def _():
        send_cm.wait_send()

    @pl.when(pos < last)
    def _():
        for step in range(1, SPAN):
            share_cm(step).wait_send()
        for l in range(2):
            handed(*we_args(l))


def on_device(cuts, energies, inverse, coupling, pattern, source, previous, offsets, strength):
    no, nr = source.shape[4], source.shape[3]
    blocks = pattern.shape[-1]
    width = nr // PARTS
    dma = pltpu.SemaphoreType.DMA
    panel = pltpu.VMEM((2, 2, nr, no), BF16)
    stack = pltpu.VMEM((blocks, 2 * no // blocks, no), BF16)
    anywhere = pl.BlockSpec(memory_space=pl.ANY)
    scalars = pl.BlockSpec(memory_space=pltpu.SMEM)
    return pl.pallas_call(
        functools.partial(sweep_kernel, cuts, energies),
        name="sweeps",
        out_shape=jax.ShapeDtypeStruct(source.shape, BF16),
        in_specs=[anywhere, anywhere, scalars, anywhere, anywhere, scalars, scalars],
        out_specs=anywhere,
        scratch_shapes=[
            pltpu.VMEM((2, 2, no, no), BF16),
            pltpu.VMEM((2, no, 2 * no), BF16),
            pltpu.VMEM((2, no, no), BF16),
            stack, stack, stack,
            pltpu.VMEM((2, no, 2 * no), BF16),
            pltpu.VMEM((2, no, 2 * no), BF16),
            pltpu.VMEM((SPAN, no, 2 * no), BF16),
            pltpu.VMEM((SPAN, no, 2 * no), BF16),
            panel, panel, panel, panel,
            pltpu.VMEM((PARTS, 2, 2, width, no), BF16),
            pltpu.VMEM((PARTS, SPAN + 1, 2, width, no), BF16),
            pltpu.VMEM((PARTS, SPAN + 1, 2, width, no), BF16),
            dma((5,)),
            dma((PARTS,)), dma((PARTS,)), dma((PARTS,)), dma((PARTS,)),
            dma, dma,
            dma((SPAN - 1,)), dma((SPAN - 1,)),
            dma((2,)), dma((SPAN,)), dma((2,)), dma((SPAN,)),
            dma((2 * PARTS,)), dma((SPAN * PARTS,)),
            dma((PARTS,)), dma((PARTS,)), dma((PARTS,)), dma((PARTS,)),
            dma((SPAN * PARTS,)), dma((2 * PARTS,)),
        ],
        compiler_params=pltpu.CompilerParams(
            collective_id=0, has_side_effects=True, vmem_limit_bytes=60 << 20
        ),
    )(inverse, coupling, pattern, source, previous, offsets, strength)


def solution(mesh):
    return jax.shard_map(
        functools.partial(on_device, mesh.shape["cuts"], mesh.shape["energy"]),
        mesh=mesh,
        in_specs=(
            P(None, "energy", "cuts", None, None),
            P(None, "cuts", None, None),
            P("cuts", None, None),
            P(None, "energy", "cuts", None, None),
            P(None, "energy", "cuts", None, None),
            P(),
            P(),
        ),
        out_specs=P(None, "energy", "cuts", None, None),
        check_vma=False,
    )
```

time: 813 us -> 92.2 us (0.11)
  the two profiles are of different devices: /device:TPU:6 before, /device:TPU:1 now
where the time goes in v2:
time: 92.2 us; the launch traced here: 92 us
  Pallas kernels  90.2 us (98%)
  local copies, waits for them, and re-layouts  1.77 us (2%)
    pallas_call x1, Pallas kernels, on_device(): pl.pallas_call(functools.partial(sweep_kernel, cuts, energies), name='swe...  90.2 us

profile of v2, /device:TPU:1, one launch (start us, length us, event | category | flops | bytes accessed | tf_op | source)
XLA Modules:
  0.0 92.0 jit_solution(1149725588451441494)
XLA Ops:
  0.0 90.2 %sweeps.1 = bf16[2,2,1,96,512]{4,3,2,1,0:T(8,128)(2,1)} custom-call(bf16[2,2,1,512,512]{4,3,2,1,0:T(8,128)(2,1)} %inv_ref.1, bf16[2,1,512,512]{3,2,1,0:T(8,128)(2,1)} %cpl_ref.1, s32[1,4,4]{2,1,0:T(4,128)} %pat_ref.1, bf16[2,2,1,96,512]{4,3,2,1,0:T(8,128)(2,1)} %src_ref.1, bf16[2,2,1,96,512]{4,3,2,1,0:T(8,128)(2,1)} %prev_ref.1, s32[4]{0:T(128)} %off_ref.1, ...), custom_call_target="tpu_custom_call" | custom-call | tf_op jit(solution)/shard_map/sweeps/pallas_call | solution.py:385
  90.2 1.8 %copy.9 = bf16[2,2,1,96,512]{4,3,2,1,0:T(8,128)(2,1)} copy(bf16[2,2,1,96,512]{4,3,2,1,0:T(8,128)(2,1)} %sweeps.1) | data formatting | bytes 786432

commit v3 on v2

--- a/solution.py
+++ b/solution.py
@@ -25,7 +25,7 @@
     cuts, energies, inv_ref, cpl_ref, pat_ref, src_ref, prev_ref, off_ref, str_ref, out_ref,
     inv_v, it_v, cpl_v, cm_v, cmt_v, cm1_v, wfo_v, weo_v, wf_v, we_v, src_v, prev_v, hl_v, hr_v,
     ao_v, x_v, u_v,
-    load_sem, hs_l, hs_r, hr_l, hr_r, cm_s, cm_r, cx_s, cx_r, wf_s, wf_r, we_s, we_r, a_s, a_r,
+    load_sem, hs_l, hs_r, hr_l, hr_r, cm_s, cm_r, cx_s, cx_r, cc_s, cc_r, wf_s, wf_r, we_s, we_r, a_s, a_r,
     f_s, f_r, b_s, b_r, o_s, o_r,
 ):
     blocks = pat_ref.shape[-1]
@@ -87,22 +87,12 @@
         @pl.when(there)
         def _():
             pl.semaphore_signal(barrier, inc=1, device_id=device, device_id_type=MESH)
-    pl.semaphore_wait(barrier, sum(jnp.where(there, 1, 0) for there, _ in partners))
 
     def halo_right(c):
         return remote(prev_ref.at[:, :, 0, rows(c)], hl_v.at[:, :, rows(c)], hs_r.at[c], hr_l.at[c], {"energy": e + 1})
 
     def halo_left(c):
         return remote(prev_ref.at[:, :, 0, rows(c)], hr_v.at[:, :, rows(c)], hs_l.at[c], hr_r.at[c], {"energy": e - 1})
-
-    for c in range(PARTS):
-        @pl.when(e < energies - 1)
-        def _():
-            halo_right(c).start()
-
-        @pl.when(e > 0)
-        def _():
-            halo_left(c).start()
 
     load_cpl.wait()
     for a in range(blocks):
@@ -114,18 +104,24 @@
             cm_v[a, :nb, lanes] = (real * (-keep)).astype(BF16)
             cm_v[a, nb:, lanes] = (imag * keep).astype(BF16)
 
-    send_cm = remote(cm_v.at[x], cm1_v.at[x], cm_s, cm_r, {"cuts": pos - 1})
+    half = pl.ds(pl.multiple_of(core * nb, nb), nb)
+    send_cm = remote(cm_v.at[x, half], cm1_v.at[x, half], cm_s, cm_r, {"cuts": pos - 1})
 
     def share_cm(step):
-        return remote(cm1_v.at[x], cm1_v.at[x], cx_s.at[step - 1], cx_r.at[step - 1], x_peer(step))
+        return remote(cm1_v.at[x, half], cm1_v.at[x, half], cx_s.at[step - 1], cx_r.at[step - 1], x_peer(step))
 
     def shared_cm(step):
         slot = lax.rem(x + SPAN - step, SPAN)
-        return remote(cm1_v.at[slot], cm1_v.at[slot], cx_s.at[step - 1], cx_r.at[step - 1], x_peer(step))
-
-    @pl.when(pos > 0)
-    def _():
-        send_cm.start()
+        return remote(
+            cm1_v.at[slot, half], cm1_v.at[slot, half], cx_s.at[step - 1], cx_r.at[step - 1], x_peer(step)
+        )
+
+    mate_cm = remote(cm1_v.at[:, half], cm1_v.at[:, half], cc_s, cc_r, {"energy": first_e + 1 - core})
+
+    def pool_cm():
+        for step in range(1, SPAN):
+            shared_cm(step).wait_recv()
+        mate_cm.start()
 
     for l in range(2):
         load_inv[l].wait()
@@ -133,13 +129,11 @@
         it_v[l, :, no:] = inv_v[l, 1].T
 
     def product_into(left, l, target):
-        @pl.loop(0, blocks)
-        def _(t):
-            product = jnp.dot(left[t], it_v[l], preferred_element_type=F32)
-            real, imag = combined(product)
-            top = pl.ds(pl.multiple_of(t * nb, nb), nb)
-            target[l, top, :no] = real.astype(BF16)
-            target[l, top, no:] = imag.astype(BF16)
+        product = jnp.dot(left[...].reshape(2 * no, no), it_v[l], preferred_element_type=F32)
+        for t in range(blocks):
+            real, imag = combined(product[2 * nb * t:2 * nb * (t + 1)])
+            target[l, nb * t:nb * (t + 1), :no] = real.astype(BF16)
+            target[l, nb * t:nb * (t + 1), no:] = imag.astype(BF16)
 
     def owner(l):
         return {"cuts": base + 2 * core + l, "energy": first_e + 1}
@@ -183,6 +177,25 @@
         @pl.loop(0, 2)
         def _(l):
             product_into(cmt_v, l, wfo_v)
+
+    pl.semaphore_wait(barrier, sum(jnp.where(there, 1, 0) for there, _ in partners))
+
+    @pl.when(pos > 0)
+    def _():
+        send_cm.start()
+
+    for c in range(PARTS):
+        @pl.when(e < energies - 1)
+        def _():
+            halo_right(c).start()
+
+        @pl.when(e > 0)
+        def _():
+            halo_left(c).start()
+
+    @pl.when(pos > 0)
+    def _():
+        for l in range(2):
             hand(*wf_args(l))
 
     @pl.when(pos < last)
@@ -190,6 +203,10 @@
         send_cm.wait_recv()
         for step in range(1, SPAN):
             share_cm(step).start()
+
+    @pl.when((pos < last) & (place < SPAN - 1))
+    def _():
+        pool_cm()
 
     near = F32(0)
     far = F32(0)
@@ -232,10 +249,13 @@
             ao_v[c, l, 1] = imag.astype(BF16)
             hand(*a_args(c, l))
 
+    @pl.when((pos < last) & (place == SPAN - 1))
+    def _():
+        pool_cm()
+
     @pl.when(pos < last)
     def _():
-        for step in range(1, SPAN):
-            shared_cm(step).wait_recv()
+        mate_cm.wait_recv()
 
         @pl.loop(0, 2)
         def _(l):
@@ -369,6 +389,7 @@
     def _():
         for step in range(1, SPAN):
             share_cm(step).wait_send()
+        mate_cm.wait_send()
         for l in range(2):
             handed(*we_args(l))
 
@@ -405,6 +426,7 @@
             dma((PARTS,)), dma((PARTS,)), dma((PARTS,)), dma((PARTS,)),
             dma, dma,
             dma((SPAN - 1,)), dma((SPAN - 1,)),
+            dma, dma,
             dma((2,)), dma((SPAN,)), dma((2,)), dma((SPAN,)),
             dma((2 * PARTS,)), dma((SPAN * PARTS,)),
             dma((PARTS,)), dma((PARTS,)), dma((PARTS,)), dma((PARTS,)),

time: 92.2 us -> 88.6 us (0.961)
  Pallas kernels: 90.2 us -> 86.7 us
    pallas_call x1, Pallas kernels: 90.2 us -> 86.7 us  [on_device(): pl.pallas_call(functools.partial(sweep_kernel, cuts, energies), name='swe...]
where the time goes in v3:
time: 88.6 us; the launch traced here: 88.4 us
  Pallas kernels  86.7 us (98%)
  local copies, waits for them, and re-layouts  1.77 us (2%)
    pallas_call x1, Pallas kernels, on_device(): pl.pallas_call(functools.partial(sweep_kernel, cuts, energies), name='swe...  86.7 us

profile of v3, /device:TPU:1, one launch (start us, length us, event | category | flops | bytes accessed | tf_op | source)
XLA Modules:
  0.0 88.4 jit_solution(6149634514063539115)
XLA Ops:
  0.0 86.7 %sweeps.1 = bf16[2,2,1,96,512]{4,3,2,1,0:T(8,128)(2,1)} custom-call(bf16[2,2,1,512,512]{4,3,2,1,0:T(8,128)(2,1)} %inv_ref.1, bf16[2,1,512,512]{3,2,1,0:T(8,128)(2,1)} %cpl_ref.1, s32[1,4,4]{2,1,0:T(4,128)} %pat_ref.1, bf16[2,2,1,96,512]{4,3,2,1,0:T(8,128)(2,1)} %src_ref.1, bf16[2,2,1,96,512]{4,3,2,1,0:T(8,128)(2,1)} %prev_ref.1, s32[4]{0:T(128)} %off_ref.1, ...), custom_call_target="tpu_custom_call" | custom-call | tf_op jit(solution)/shard_map/sweeps/pallas_call | solution.py:406
  86.7 1.8 %copy.9 = bf16[2,2,1,96,512]{4,3,2,1,0:T(8,128)(2,1)} copy(bf16[2,2,1,96,512]{4,3,2,1,0:T(8,128)(2,1)} %sweeps.1) | data formatting | bytes 786432

commit v4 on v3

--- a/solution.py
+++ b/solution.py
@@ -23,9 +23,9 @@
 
 def sweep_kernel(
     cuts, energies, inv_ref, cpl_ref, pat_ref, src_ref, prev_ref, off_ref, str_ref, out_ref,
-    inv_v, it_v, cpl_v, cm_v, cmt_v, cm1_v, wfo_v, weo_v, wf_v, we_v, src_v, prev_v, hl_v, hr_v,
+    inv_v, it_v, cpl_v, cm_v, cmt_v, cmr_v, wfo_v, weo_v, wf_v, we_v, itr_v, src_v, prev_v, hl_v, hr_v,
     ao_v, x_v, u_v,
-    load_sem, hs_l, hs_r, hr_l, hr_r, cm_s, cm_r, cx_s, cx_r, cc_s, cc_r, wf_s, wf_r, we_s, we_r, a_s, a_r,
+    load_sem, hs_l, hs_r, hr_l, hr_r, cm_s, cm_r, ring_s, ring_r, cx_s, cx_r, cc_s, cc_r, fw_s, fw_r, fe_s, wf_s, wf_r, we_s, we_r, a_s, a_r,
     f_s, f_r, b_s, b_r, o_s, o_r,
 ):
     blocks = pat_ref.shape[-1]
@@ -39,9 +39,11 @@
     last = cuts - 1
     place = lax.rem(pos, SPAN)
     base = pos - place
-    xs = energies // SPAN
-    stride = xs
+    stride = energies // SPAN
     x = lax.div(e, stride)
+    late = base >= cuts // 2
+    early = base < cuts // 2
+    final_group = base == cuts - SPAN
 
     def rows(c):
         return pl.ds(c * width, width)
@@ -105,35 +107,47 @@
             cm_v[a, nb:, lanes] = (imag * keep).astype(BF16)
 
     half = pl.ds(pl.multiple_of(core * nb, nb), nb)
-    send_cm = remote(cm_v.at[x, half], cm1_v.at[x, half], cm_s, cm_r, {"cuts": pos - 1})
-
-    def share_cm(step):
-        return remote(cm1_v.at[x, half], cm1_v.at[x, half], cx_s.at[step - 1], cx_r.at[step - 1], x_peer(step))
-
-    def shared_cm(step):
-        slot = lax.rem(x + SPAN - step, SPAN)
-        return remote(
-            cm1_v.at[slot, half], cm1_v.at[slot, half], cx_s.at[step - 1], cx_r.at[step - 1], x_peer(step)
-        )
-
-    mate_cm = remote(cm1_v.at[:, half], cm1_v.at[:, half], cc_s, cc_r, {"energy": first_e + 1 - core})
-
-    def pool_cm():
+    send_cm = remote(cm_v.at[x, half], cmr_v.at[SPAN, x, half], cm_s, cm_r, {"cuts": pos - 1})
+    shifts_out = (pos > 0) & (pos <= cuts // 2)
+
+    def in_ring(step):
+        return {"cuts": base + lax.rem(place + step, SPAN)}
+
+    def ring_cm(step):
+        return remote(cm_v.at[x, half], cmr_v.at[place, x, half], ring_s.at[step - 1], ring_r.at[place], in_ring(step))
+
+    def ringed_cm(slot):
+        return remote(cm_v.at[x, half], cmr_v.at[slot, x, half], ring_s.at[0], ring_r.at[slot], in_ring(1))
+
+    def share_cm(slot, step):
+        piece = cmr_v.at[slot, x, half]
+        n = (SPAN - 1) * slot + step - 1
+        return remote(piece, piece, cx_s.at[n], cx_r.at[n], x_peer(step))
+
+    def shared_cm(slot, step):
+        piece = cmr_v.at[slot, lax.rem(x + SPAN - step, SPAN), half]
+        n = (SPAN - 1) * slot + step - 1
+        return remote(piece, piece, cx_s.at[n], cx_r.at[n], x_peer(step))
+
+    def mate_cm(slot):
+        piece = cmr_v.at[slot, :, half]
+        return remote(piece, piece, cc_s.at[slot], cc_r.at[slot], {"energy": first_e + 1 - core})
+
+    def pool_cm(slot):
         for step in range(1, SPAN):
-            shared_cm(step).wait_recv()
-        mate_cm.start()
+            shared_cm(slot, step).wait_recv()
 
     for l in range(2):
         load_inv[l].wait()
         it_v[l, :, :no] = inv_v[l, 0].T
         it_v[l, :, no:] = inv_v[l, 1].T
 
-    def product_into(left, l, target):
-        product = jnp.dot(left[...].reshape(2 * no, no), it_v[l], preferred_element_type=F32)
+    def product_into(left, right, target):
+        product = jnp.dot(left[...].reshape(2 * no, no), right[...], preferred_element_type=F32)
         for t in range(blocks):
             real, imag = combined(product[2 * nb * t:2 * nb * (t + 1)])
-            target[l, nb * t:nb * (t + 1), :no] = real.astype(BF16)
-            target[l, nb * t:nb * (t + 1), no:] = imag.astype(BF16)
+            target[nb * t:nb * (t + 1), :no] = real.astype(BF16)
+            target[nb * t:nb * (t + 1), no:] = imag.astype(BF16)
 
     def owner(l):
         return {"cuts": base + 2 * core + l, "energy": first_e + 1}
@@ -161,28 +175,43 @@
     def we_args(l):
         return weo_v.at[l], we_v.at[place], l, we_s.at[l], we_r.at[place]
 
+    def it_args(l):
+        return it_v.at[l], itr_v.at[place], l, wf_s.at[l], wf_r.at[place]
+
     def a_args(c, l):
         return ao_v.at[c, l], x_v.at[c, 1 + place], l, a_s.at[2 * c + l], a_r.at[PARTS * place + c]
 
-    @pl.when(pos > 0)
-    def _():
+    def turn(given):
         for t in range(blocks):
             lanes = slice(t * nb, (t + 1) * nb)
-            real = cm_v[t, :nb, :].T
-            imag = -(cm_v[t, nb:, :].T)
+            real = given[t, :nb, :].T
+            imag = -(given[t, nb:, :].T)
             for s in range(blocks):
                 cmt_v[s, :nb, lanes] = real[s * nb:(s + 1) * nb]
                 cmt_v[s, nb:, lanes] = imag[s * nb:(s + 1) * nb]
 
+    @pl.when((pos > 0) & early)
+    def _():
+        turn(cm_v)
+
         @pl.loop(0, 2)
         def _(l):
-            product_into(cmt_v, l, wfo_v)
+            product_into(cmt_v, it_v.at[l], wfo_v.at[l])
+
+    @pl.when(late)
+    def _():
+        cmr_v[place] = cm_v[...]
 
     pl.semaphore_wait(barrier, sum(jnp.where(there, 1, 0) for there, _ in partners))
 
-    @pl.when(pos > 0)
+    @pl.when(shifts_out)
     def _():
         send_cm.start()
+
+    @pl.when(late)
+    def _():
+        for step in range(1, SPAN):
+            ring_cm(step).start()
 
     for c in range(PARTS):
         @pl.when(e < energies - 1)
@@ -193,20 +222,32 @@
         def _():
             halo_left(c).start()
 
-    @pl.when(pos > 0)
+    @pl.when((pos > 0) & early)
     def _():
         for l in range(2):
             hand(*wf_args(l))
 
-    @pl.when(pos < last)
+    @pl.when(late)
+    def _():
+        for slot in range(SPAN):
+            @pl.when(slot != place)
+            def _():
+                ringed_cm(slot).wait_recv()
+                for step in range(1, SPAN):
+                    share_cm(slot, step).start()
+        for l in range(2):
+            hand(*it_args(l))
+
+    @pl.when(early)
     def _():
         send_cm.wait_recv()
         for step in range(1, SPAN):
-            share_cm(step).start()
-
-    @pl.when((pos < last) & (place < SPAN - 1))
-    def _():
-        pool_cm()
+            share_cm(SPAN, step).start()
+
+    @pl.when(early & (place < SPAN - 1))
+    def _():
+        pool_cm(SPAN)
+        mate_cm(SPAN).start()
 
     near = F32(0)
     far = F32(0)
@@ -249,27 +290,82 @@
             ao_v[c, l, 1] = imag.astype(BF16)
             hand(*a_args(c, l))
 
-    @pl.when((pos < last) & (place == SPAN - 1))
-    def _():
-        pool_cm()
-
-    @pl.when(pos < last)
-    def _():
-        mate_cm.wait_recv()
+    @pl.when(early & (place == SPAN - 1))
+    def _():
+        pool_cm(SPAN)
+        mate_cm(SPAN).start()
+
+    @pl.when(early)
+    def _():
+        mate_cm(SPAN).wait_recv()
 
         @pl.loop(0, 2)
         def _(l):
-            product_into(cm1_v, l, weo_v)
-
-    @pl.when(pos > 0)
+            product_into(cmr_v.at[SPAN], it_v.at[l], weo_v.at[l])
+
+    @pl.when((pos > 0) & early)
     def _():
         for l in range(2):
             handed(*wf_args(l))
 
-    @pl.when(pos < last)
+    @pl.when(early)
     def _():
         for l in range(2):
             hand(*we_args(l))
+
+    @pl.when(late)
+    def _():
+        for slot in range(SPAN):
+            @pl.when(slot != place)
+            def _():
+                pool_cm(slot)
+                mate_cm(slot).start()
+
+        for slot in range(SPAN):
+            @pl.when(slot != place)
+            def _():
+                mate_cm(slot).wait_recv()
+
+    def pass_on(j):
+        return remote(itr_v.at[j], itr_v.at[j], fw_s.at[j], fw_r.at[j], {"energy": first_e + 1 - core})
+
+    def pass_back(j):
+        return remote(we_v.at[j], we_v.at[j], fe_s.at[j], we_r.at[j], {"energy": first_e + 1 - core})
+
+    @pl.when(late & (core == 1))
+    def _():
+        @pl.loop(0, SPAN)
+        def _(back):
+            j = SPAN - 1 - back
+            remote(it_v.at[0], itr_v.at[j], wf_s.at[0], wf_r.at[j], owner(0)).wait_recv()
+
+            @pl.when(j < SPAN - 1)
+            def _():
+                pass_on(j).start()
+
+        @pl.loop(0, SPAN)
+        def _(j):
+            turn(cmr_v.at[j])
+            product_into(cmt_v, itr_v.at[j], wf_v.at[j])
+
+        @pl.when(final_group)
+        def _():
+            for t in range(blocks):
+                we_v[SPAN - 1, nb * t:nb * (t + 1), :no] = cmr_v[0, t, :nb]
+                we_v[SPAN - 1, nb * t:nb * (t + 1), no:] = cmr_v[0, t, nb:]
+
+        @pl.when(jnp.logical_not(final_group))
+        def _():
+            we_v[SPAN - 1] = itr_v[SPAN - 1]
+
+    @pl.when(late & (core == 0))
+    def _():
+        @pl.loop(0, SPAN - 1)
+        def _(back):
+            j = SPAN - 2 - back
+            pass_on(j).wait_recv()
+            product_into(cmr_v.at[j + 1], itr_v.at[j], we_v.at[j])
+            pass_back(j).start()
 
     def stepped(given, weights, added):
         left = given[...].reshape(2 * width, no)
@@ -282,6 +378,9 @@
     def send_backward(c):
         return remote(u_v.at[c, 0], u_v.at[c, SPAN], b_s.at[c], b_r.at[c], {"cuts": pos - SPAN})
 
+    def send_coupled(c):
+        return remote(x_v.at[c, 0], u_v.at[c, SPAN], b_s.at[c], b_r.at[c], {"cuts": pos - SPAN})
+
     def out_at(c, l):
         return out_ref.at[:, l, 0, rows(c)]
 
@@ -311,7 +410,10 @@
                 @pl.when(base + j > 0)
                 def _():
                     if c == 0:
-                        remote(wfo_v.at[0], wf_v.at[j], wf_s.at[0], wf_r.at[j], owner(0)).wait_recv()
+                        @pl.when(early)
+                        def _():
+                            remote(wfo_v.at[0], wf_v.at[j], wf_s.at[0], wf_r.at[j], owner(0)).wait_recv()
+
                     here = x_v.at[c, 1 + j]
                     here[0], here[1] = stepped(x_v.at[c, j], wf_v.at[j], here)
 
@@ -331,7 +433,10 @@
                 @pl.when(base + j < last)
                 def _():
                     if c == 0:
-                        remote(weo_v.at[0], we_v.at[j], we_s.at[0], we_r.at[j], owner(0)).wait_recv()
+                        @pl.when(early | (back > 0))
+                        def _():
+                            remote(weo_v.at[0], we_v.at[j], we_s.at[0], we_r.at[j], owner(0)).wait_recv()
+
                     here = u_v.at[c, j]
                     here[0], here[1] = stepped(u_v.at[c, j + 1], we_v.at[j], x_v.at[c, 1 + j])
 
@@ -339,9 +444,17 @@
                 def _():
                     u_v[c, j] = x_v[c, 1 + j]
 
-                @pl.when((j == 0) & (base > 0))
+                @pl.when((j == 0) & (base > 0) & jnp.logical_not(final_group))
                 def _():
                     send_backward(c).start()
+
+                @pl.when((j == 0) & final_group)
+                def _():
+                    left = u_v[c, 0].reshape(2 * width, no)
+                    real, imag = combined(jnp.dot(left, we_v[SPAN - 1], preferred_element_type=F32))
+                    x_v[c, 0, 0] = real.astype(BF16)
+                    x_v[c, 0, 1] = imag.astype(BF16)
+                    send_coupled(c).start()
 
                 for l in range(2):
                     @pl.when((half_place == l) & is_home(j))
@@ -381,18 +494,44 @@
         def _():
             halo_left(c).wait_send()
 
-    @pl.when(pos > 0)
+    @pl.when(shifts_out)
     def _():
         send_cm.wait_send()
 
-    @pl.when(pos < last)
+    @pl.when(early)
     def _():
         for step in range(1, SPAN):
-            share_cm(step).wait_send()
-        mate_cm.wait_send()
+            share_cm(SPAN, step).wait_send()
+        mate_cm(SPAN).wait_send()
+
+    @pl.when(early)
+    def _():
         for l in range(2):
             handed(*we_args(l))
 
+    @pl.when(late)
+    def _():
+        for step in range(1, SPAN):
+            ring_cm(step).wait_send()
+        for l in range(2):
+            handed(*it_args(l))
+        for slot in range(SPAN):
+            @pl.when(slot != place)
+            def _():
+                for step in range(1, SPAN):
+                    share_cm(slot, step).wait_send()
+
+                mate_cm(slot).wait_send()
+
+        @pl.loop(0, SPAN - 1)
+        def _(j):
+            @pl.when(core == 1)
+            def _():
+                pass_on(j).wait_send()
+
+            @pl.when(core == 0)
+            def _():
+                pass_back(j).wait_send()
 
 def on_device(cuts, energies, inverse, coupling, pattern, source, previous, offsets, strength):
     no, nr = source.shape[4], source.shape[3]
@@ -413,9 +552,11 @@
             pltpu.VMEM((2, 2, no, no), BF16),
             pltpu.VMEM((2, no, 2 * no), BF16),
             pltpu.VMEM((2, no, no), BF16),
-            stack, stack, stack,
+            stack, stack,
+            pltpu.VMEM((SPAN + 1, blocks, 2 * no // blocks, no), BF16),
             pltpu.VMEM((2, no, 2 * no), BF16),
             pltpu.VMEM((2, no, 2 * no), BF16),
+            pltpu.VMEM((SPAN, no, 2 * no), BF16),
             pltpu.VMEM((SPAN, no, 2 * no), BF16),
             pltpu.VMEM((SPAN, no, 2 * no), BF16),
             panel, panel, panel, panel,
@@ -425,8 +566,10 @@
             dma((5,)),
             dma((PARTS,)), dma((PARTS,)), dma((PARTS,)), dma((PARTS,)),
             dma, dma,
-            dma((SPAN - 1,)), dma((SPAN - 1,)),
-            dma, dma,
+            dma((SPAN - 1,)), dma((SPAN,)),
+            dma(((SPAN - 1) * (SPAN + 1),)), dma(((SPAN - 1) * (SPAN + 1),)),
+            dma((SPAN + 1,)), dma((SPAN + 1,)),
+            dma((SPAN - 1,)), dma((SPAN - 1,)), dma((SPAN - 1,)),
             dma((2,)), dma((SPAN,)), dma((2,)), dma((SPAN,)),
             dma((2 * PARTS,)), dma((SPAN * PARTS,)),
             dma((PARTS,)), dma((PARTS,)), dma((PARTS,)), dma((PARTS,)),

time: 88.6 us -> 83.9 us (0.947)
  Pallas kernels: 86.7 us -> 81.9 us
    pallas_call x1, Pallas kernels: 86.7 us -> 81.9 us  [on_device(): pl.pallas_call(functools.partial(sweep_kernel, cuts, energies), name='swe...]
where the time goes in v4:
time: 83.9 us; the launch traced here: 83.7 us
  Pallas kernels  81.9 us (98%)
  local copies, waits for them, and re-layouts  1.77 us (2%)
    pallas_call x1, Pallas kernels, on_device(): pl.pallas_call(functools.partial(sweep_kernel, cuts, energies), name='swe...  81.9 us
    unnamed x1, local copies, waits for them, and re-layouts  1.77 us

profile of v4, /device:TPU:1, one launch (start us, length us, event | category | flops | bytes accessed | tf_op | source)
XLA Modules:
  0.0 83.7 jit_solution(8398053320487226350)
XLA Ops:
  0.0 81.9 %sweeps.1 = bf16[2,2,1,96,512]{4,3,2,1,0:T(8,128)(2,1)} custom-call(bf16[2,2,1,512,512]{4,3,2,1,0:T(8,128)(2,1)} %inv_ref.1, bf16[2,1,512,512]{3,2,1,0:T(8,128)(2,1)} %cpl_ref.1, s32[1,4,4]{2,1,0:T(4,128)} %pat_ref.1, bf16[2,2,1,96,512]{4,3,2,1,0:T(8,128)(2,1)} %src_ref.1, bf16[2,2,1,96,512]{4,3,2,1,0:T(8,128)(2,1)} %prev_ref.1, s32[4]{0:T(128)} %off_ref.1, ...), custom_call_target="tpu_custom_call" | custom-call | tf_op jit(solution)/shard_map/sweeps/pallas_call | solution.py:545
  81.9 1.8 %copy.9 = bf16[2,2,1,96,512]{4,3,2,1,0:T(8,128)(2,1)} copy(bf16[2,2,1,96,512]{4,3,2,1,0:T(8,128)(2,1)} %sweeps.1) | data formatting | bytes 786432

commit v5 on v4

--- a/solution.py
+++ b/solution.py
@@ -155,6 +155,9 @@
     def is_owner(l):
         return (core == 1) & (place == 2 + l)
 
+    def is_far(l):
+        return lax.rem(2 * core + l - place + SPAN, SPAN) == 2
+
     def hand(src, dst, l, send, recv):
         @pl.when(is_owner(l))
         def _():
@@ -229,15 +232,22 @@
 
     @pl.when(late)
     def _():
+        for l in range(2):
+            @pl.when(jnp.logical_not(is_far(l)))
+            def _():
+                hand(*it_args(l))
+
+        for l in range(2):
+            @pl.when(is_far(l))
+            def _():
+                hand(*it_args(l))
+
         for slot in range(SPAN):
             @pl.when(slot != place)
             def _():
                 ringed_cm(slot).wait_recv()
                 for step in range(1, SPAN):
                     share_cm(slot, step).start()
-        for l in range(2):
-            hand(*it_args(l))
-
     @pl.when(early)
     def _():
         send_cm.wait_recv()
@@ -303,11 +313,6 @@
         def _(l):
             product_into(cmr_v.at[SPAN], it_v.at[l], weo_v.at[l])
 
-    @pl.when((pos > 0) & early)
-    def _():
-        for l in range(2):
-            handed(*wf_args(l))
-
     @pl.when(early)
     def _():
         for l in range(2):
@@ -326,6 +331,9 @@
             def _():
                 mate_cm(slot).wait_recv()
 
+    def by_arrival(n):
+        return lax.rem(place + jnp.where(n < 2, n, 5 - n), SPAN)
+
     def pass_on(j):
         return remote(itr_v.at[j], itr_v.at[j], fw_s.at[j], fw_r.at[j], {"energy": first_e + 1 - core})
 
@@ -335,16 +343,14 @@
     @pl.when(late & (core == 1))
     def _():
         @pl.loop(0, SPAN)
-        def _(back):
-            j = SPAN - 1 - back
+        def _(turn_no):
+            j = by_arrival(turn_no)
             remote(it_v.at[0], itr_v.at[j], wf_s.at[0], wf_r.at[j], owner(0)).wait_recv()
 
             @pl.when(j < SPAN - 1)
             def _():
                 pass_on(j).start()
 
-        @pl.loop(0, SPAN)
-        def _(j):
             turn(cmr_v.at[j])
             product_into(cmt_v, itr_v.at[j], wf_v.at[j])
 
@@ -360,12 +366,15 @@
 
     @pl.when(late & (core == 0))
     def _():
-        @pl.loop(0, SPAN - 1)
-        def _(back):
-            j = SPAN - 2 - back
-            pass_on(j).wait_recv()
-            product_into(cmr_v.at[j + 1], itr_v.at[j], we_v.at[j])
-            pass_back(j).start()
+        @pl.loop(0, SPAN)
+        def _(turn_no):
+            j = by_arrival(turn_no)
+
+            @pl.when(j < SPAN - 1)
+            def _():
+                pass_on(j).wait_recv()
+                product_into(cmr_v.at[j + 1], itr_v.at[j], we_v.at[j])
+                pass_back(j).start()
 
     def stepped(given, weights, added):
         left = given[...].reshape(2 * width, no)
@@ -503,6 +512,11 @@
         for step in range(1, SPAN):
             share_cm(SPAN, step).wait_send()
         mate_cm(SPAN).wait_send()
+
+    @pl.when((pos > 0) & early)
+    def _():
+        for l in range(2):
+            handed(*wf_args(l))
 
     @pl.when(early)
     def _():

time: 83.9 us -> 81.2 us (0.968)
  the two profiles are of different devices: /device:TPU:1 before, /device:TPU:14 now
where the time goes in v5:
time: 81.2 us; the launch traced here: 81 us
  Pallas kernels  79.3 us (98%)
  local copies, waits for them, and re-layouts  1.77 us (2%)
    pallas_call x1, Pallas kernels, on_device(): pl.pallas_call(functools.partial(sweep_kernel, cuts, energies), name='swe...  79.3 us
    unnamed x1, local copies, waits for them, and re-layouts  1.77 us

profile of v5, /device:TPU:14, one launch (start us, length us, event | category | flops | bytes accessed | tf_op | source)
XLA Modules:
  0.0 81.0 jit_solution(6820745691876020505)
XLA Ops:
  0.0 79.3 %sweeps.1 = bf16[2,2,1,96,512]{4,3,2,1,0:T(8,128)(2,1)} custom-call(bf16[2,2,1,512,512]{4,3,2,1,0:T(8,128)(2,1)} %inv_ref.1, bf16[2,1,512,512]{3,2,1,0:T(8,128)(2,1)} %cpl_ref.1, s32[1,4,4]{2,1,0:T(4,128)} %pat_ref.1, bf16[2,2,1,96,512]{4,3,2,1,0:T(8,128)(2,1)} %src_ref.1, bf16[2,2,1,96,512]{4,3,2,1,0:T(8,128)(2,1)} %prev_ref.1, s32[4]{0:T(128)} %off_ref.1, ...), custom_call_target="tpu_custom_call" | custom-call | tf_op jit(solution)/shard_map/sweeps/pallas_call | solution.py:559
  79.3 1.8 %copy.9 = bf16[2,2,1,96,512]{4,3,2,1,0:T(8,128)(2,1)} copy(bf16[2,2,1,96,512]{4,3,2,1,0:T(8,128)(2,1)} %sweeps.1) | data formatting | bytes 786432

commit v6 on v5

--- a/solution.py
+++ b/solution.py
@@ -137,10 +137,23 @@
         for step in range(1, SPAN):
             shared_cm(slot, step).wait_recv()
 
-    for l in range(2):
+    def load_it(l):
         load_inv[l].wait()
         it_v[l, :, :no] = inv_v[l, 0].T
         it_v[l, :, no:] = inv_v[l, 1].T
+
+    def is_far(l):
+        return lax.rem(2 * core + l - place + SPAN, SPAN) == 2
+
+    lead = jnp.where(is_far(1), 1, 0)
+
+    @pl.when(lead == 0)
+    def _():
+        load_it(0)
+
+    @pl.when(lead == 1)
+    def _():
+        load_it(1)
 
     def product_into(left, right, target):
         product = jnp.dot(left[...].reshape(2 * no, no), right[...], preferred_element_type=F32)
@@ -154,9 +167,6 @@
 
     def is_owner(l):
         return (core == 1) & (place == 2 + l)
-
-    def is_far(l):
-        return lax.rem(2 * core + l - place + SPAN, SPAN) == 2
 
     def hand(src, dst, l, send, recv):
         @pl.when(is_owner(l))
@@ -196,10 +206,14 @@
     @pl.when((pos > 0) & early)
     def _():
         turn(cm_v)
-
-        @pl.loop(0, 2)
-        def _(l):
-            product_into(cmt_v, it_v.at[l], wfo_v.at[l])
+        product_into(cmt_v, it_v.at[lead], wfo_v.at[lead])
+
+    @pl.when(late | (pos == 0))
+    def _():
+        for l in range(2):
+            @pl.when(lead != l)
+            def _():
+                load_it(l)
 
     @pl.when(late)
     def _():
@@ -216,19 +230,33 @@
         for step in range(1, SPAN):
             ring_cm(step).start()
 
-    for c in range(PARTS):
-        @pl.when(e < energies - 1)
-        def _():
-            halo_right(c).start()
-
-        @pl.when(e > 0)
-        def _():
-            halo_left(c).start()
+    def start_halos():
+        for c in range(PARTS):
+            @pl.when(e < energies - 1)
+            def _():
+                halo_right(c).start()
+
+            @pl.when(e > 0)
+            def _():
+                halo_left(c).start()
+
+    @pl.when(base == 0)
+    def _():
+        start_halos()
 
     @pl.when((pos > 0) & early)
     def _():
         for l in range(2):
-            hand(*wf_args(l))
+            @pl.when(lead == l)
+            def _():
+                hand(*wf_args(l))
+                load_it(1 - l)
+
+        product_into(cmt_v, it_v.at[1 - lead], wfo_v.at[1 - lead])
+        for l in range(2):
+            @pl.when(lead != l)
+            def _():
+                hand(*wf_args(l))
 
     @pl.when(late)
     def _():
@@ -242,12 +270,17 @@
             def _():
                 hand(*it_args(l))
 
+        start_halos()
         for slot in range(SPAN):
             @pl.when(slot != place)
             def _():
                 ringed_cm(slot).wait_recv()
                 for step in range(1, SPAN):
                     share_cm(slot, step).start()
+    @pl.when(base == SPAN)
+    def _():
+        start_halos()
+
     @pl.when(early)
     def _():
         send_cm.wait_recv()
@@ -310,12 +343,9 @@
         mate_cm(SPAN).wait_recv()
 
         @pl.loop(0, 2)
-        def _(l):
+        def _(n):
+            l = jnp.where(n == 0, lead, 1 - lead)
             product_into(cmr_v.at[SPAN], it_v.at[l], weo_v.at[l])
-
-    @pl.when(early)
-    def _():
-        for l in range(2):
             hand(*we_args(l))
 
     @pl.when(late)
@@ -408,8 +438,7 @@
     @pl.when(core == 1)
     def _():
         for c in range(PARTS):
-            @pl.loop(0, SPAN)
-            def _(j):
+            for j in range(SPAN):
                 remote(ao_v.at[c, 0], x_v.at[c, 1 + j], a_s.at[0], a_r.at[PARTS * j + c], owner(0)).wait_recv()
 
                 @pl.when((j == 0) & (base > 0))
@@ -417,7 +446,7 @@
                     send_forward(c).wait_recv()
 
                 @pl.when(base + j > 0)
-                def _():
+                def _(j=j):
                     if c == 0:
                         @pl.when(early)
                         def _():
@@ -431,8 +460,7 @@
                 send_forward(c).start()
 
         for c in range(PARTS):
-            @pl.loop(0, SPAN)
-            def _(back):
+            for back in range(SPAN):
                 j = SPAN - 1 - back
 
                 @pl.when((back == 0) & (base < cuts - SPAN))

time: 81.2 us -> 80 us (0.985)
  the two profiles are of different devices: /device:TPU:14 before, /device:TPU:1 now
where the time goes in v6:
time: 80 us; the launch traced here: 79.8 us
  Pallas kernels  78 us (98%)
  local copies, waits for them, and re-layouts  1.77 us (2%)
    pallas_call x1, Pallas kernels, on_device(): pl.pallas_call(functools.partial(sweep_kernel, cuts, energies), name='swe...  78 us
    unnamed x1, local copies, waits for them, and re-layouts  1.77 us

profile of v6, /device:TPU:1, one launch (start us, length us, event | category | flops | bytes accessed | tf_op | source)
XLA Modules:
  0.0 79.8 jit_solution(10141553984964489322)
XLA Ops:
  0.0 78.0 %sweeps.1 = bf16[2,2,1,96,512]{4,3,2,1,0:T(8,128)(2,1)} custom-call(bf16[2,2,1,512,512]{4,3,2,1,0:T(8,128)(2,1)} %inv_ref.1, bf16[2,1,512,512]{3,2,1,0:T(8,128)(2,1)} %cpl_ref.1, s32[1,4,4]{2,1,0:T(4,128)} %pat_ref.1, bf16[2,2,1,96,512]{4,3,2,1,0:T(8,128)(2,1)} %src_ref.1, bf16[2,2,1,96,512]{4,3,2,1,0:T(8,128)(2,1)} %prev_ref.1, s32[4]{0:T(128)} %off_ref.1, ...), custom_call_target="tpu_custom_call" | custom-call | tf_op jit(solution)/shard_map/sweeps/pallas_call | solution.py:587
  78.0 1.8 %copy.9 = bf16[2,2,1,96,512]{4,3,2,1,0:T(8,128)(2,1)} copy(bf16[2,2,1,96,512]{4,3,2,1,0:T(8,128)(2,1)} %sweeps.1) | data formatting | bytes 786432

commit v7 on v6

--- a/solution.py
+++ b/solution.py
@@ -61,10 +61,16 @@
     load_src = pltpu.make_async_copy(src_ref.at[:, :, 0], src_v, load_sem.at[3])
     load_prev = pltpu.make_async_copy(prev_ref.at[:, :, 0], prev_v, load_sem.at[4])
     load_cpl.start()
-    for copy in load_inv:
-        copy.start()
-    load_src.start()
-    load_prev.start()
+
+    def is_far(l):
+        return lax.rem(2 * core + l - place + SPAN, SPAN) == 2
+
+    lead = jnp.where(is_far(1), 1, 0)
+    for l in range(2):
+        @pl.when(lead == l)
+        def _():
+            load_inv[l].start()
+            load_inv[1 - l].start()
 
     def x_peer(step):
         return {"energy": lax.rem(x + step, SPAN) * stride + lax.rem(e, stride)}
@@ -142,11 +148,6 @@
         it_v[l, :, :no] = inv_v[l, 0].T
         it_v[l, :, no:] = inv_v[l, 1].T
 
-    def is_far(l):
-        return lax.rem(2 * core + l - place + SPAN, SPAN) == 2
-
-    lead = jnp.where(is_far(1), 1, 0)
-
     @pl.when(lead == 0)
     def _():
         load_it(0)
@@ -219,6 +220,8 @@
     def _():
         cmr_v[place] = cm_v[...]
 
+    load_src.start()
+    load_prev.start()
     pl.semaphore_wait(barrier, sum(jnp.where(there, 1, 0) for there, _ in partners))
 
     @pl.when(shifts_out)

time: 80 us -> 80 us (level)
  no operation moved by 1% of the time
where the time goes in v7:
time: 80 us; the launch traced here: 79.8 us
  Pallas kernels  78 us (98%)
  local copies, waits for them, and re-layouts  1.77 us (2%)
    pallas_call x1, Pallas kernels, on_device(): pl.pallas_call(functools.partial(sweep_kernel, cuts, energies), name='swe...  78 us
    unnamed x1, local copies, waits for them, and re-layouts  1.77 us

profile of v7, /device:TPU:1, one launch (start us, length us, event | category | flops | bytes accessed | tf_op | source)
XLA Modules:
  0.0 79.8 jit_solution(9409833933706175843)
XLA Ops:
  0.0 78.0 %sweeps.1 = bf16[2,2,1,96,512]{4,3,2,1,0:T(8,128)(2,1)} custom-call(bf16[2,2,1,512,512]{4,3,2,1,0:T(8,128)(2,1)} %inv_ref.1, bf16[2,1,512,512]{3,2,1,0:T(8,128)(2,1)} %cpl_ref.1, s32[1,4,4]{2,1,0:T(4,128)} %pat_ref.1, bf16[2,2,1,96,512]{4,3,2,1,0:T(8,128)(2,1)} %src_ref.1, bf16[2,2,1,96,512]{4,3,2,1,0:T(8,128)(2,1)} %prev_ref.1, s32[4]{0:T(128)} %off_ref.1, ...), custom_call_target="tpu_custom_call" | custom-call | tf_op jit(solution)/shard_map/sweeps/pallas_call | solution.py:590
  78.0 1.8 %copy.9 = bf16[2,2,1,96,512]{4,3,2,1,0:T(8,128)(2,1)} copy(bf16[2,2,1,96,512]{4,3,2,1,0:T(8,128)(2,1)} %sweeps.1) | data formatting | bytes 786432
